TPU v7x, 32 devices: a whole 2x2x4 slice. The times are simulated.
32 devices in a mesh: seq: 8 (over z, y), wt: 4 (over x, core).
Axes of the slice: x: 2, y: 2, z: 4, core: 2. Of those that a mesh axis runs over, the one named last changes fastest.
Arguments:
- hidden_in: bfloat16 [4, 2048, 2048], P('wt', 'seq'), may hold values from -6 to 6
- doc_starts: int32 [4, 2048], P('wt', 'seq'), may hold values from 0 to 1, as said below
- norm_gain: bfloat16 [2048], P('wt'), may hold values from 0.5 to 1.5
- in_weight: bfloat16 [2048, 8192], P('wt'), may hold values from -0.125 to 0.125
- conv_weight: bfloat16 [4096, 4], P('wt'), may hold values from -3 to 3
- conv_bias: bfloat16 [4096], P('wt'), may hold values from -3 to 3
- x_weight: bfloat16 [4096, 160], P('wt'), may hold values from -0.09375 to 0.09375
- dt_weight: bfloat16 [4096, 128], P('wt'), may hold values from -0.5 to 0.5
- dt_bias: bfloat16 [4096], P('wt'), may hold values from -11 to -2
- a_log: bfloat16 [4096, 16], P('wt'), may hold values from -5 to 2.796875
- d_skip: bfloat16 [4096], P('wt'), may hold values from 0.5 to 1.5
- out_weight: bfloat16 [4096, 2048], P('wt'), may hold values from -0.09375 to 0.09375
- grad_output: bfloat16 [4, 2048, 2048], P('wt', 'seq'), may hold values from -6 to 6
Outputs:
- output: float32 [4, 2048, 2048], P('wt', 'seq')
- input_grad: float32 [4, 2048, 2048], P('wt', 'seq')
- norm_gain_grad: float32 [2048], P(('seq', 'wt'))
- in_weight_grad: float32 [2048, 8192], P(('seq', 'wt'))
- conv_weight_grad: float32 [4096, 4], P(('seq', 'wt'))
- conv_bias_grad: float32 [4096], P(('seq', 'wt'))
- x_weight_grad: float32 [4096, 160], P(('seq', 'wt'))
- dt_weight_grad: float32 [4096, 128], P(('seq', 'wt'))
- dt_bias_grad: float32 [4096], P(('seq', 'wt'))
- a_log_grad: float32 [4096, 16], P(('seq', 'wt'))
- d_skip_grad: float32 [4096], P(('seq', 'wt'))
- out_weight_grad: float32 [4096, 2048], P(('seq', 'wt'))
Inputs may be any that keep to these rules, and one draw needn't show every extreme that they name: `doc_starts`: each stream's first position begins a document; in each stream one document begins within the first 256 positions and ends within the last 256.
All inputs are finite; a program needn't handle non-finite values.
Results may differ from a plain program's by a relative error of at most 0.0095.
Values may be sent and summed in bfloat16 or wider, within the bound.
A program may use at most 640 MiB of HBM per device.

v0:
```python
import functools
import math

import jax
import jax.numpy as jnp
import ml_dtypes
import numpy as np
from jax import lax
from jax.experimental import pallas as pl
from jax.experimental.pallas import tpu as pltpu
from jax.sharding import PartitionSpec as P

EPS = 1e-05
LOG2E = 1.4426950408889634
RESET = 1e30
SUB = 8
LANE = 128
NBLK = 4
F32 = jnp.float32
BF16 = jnp.bfloat16
MESH = pl.DeviceIdType.MESH


def softplus(v):
    return jnp.maximum(v, 0.0) + jnp.log1p(jnp.exp(-jnp.abs(v)))


def wide(tile, width):
    return jnp.concatenate([tile] * (width // LANE), axis=1)


def fold(values):
    total = values[:, :LANE]
    for k in range(1, values.shape[1] // LANE):
        total = total + values[:, k * LANE : (k + 1) * LANE]
    return total


def chunk_prefix(decay, drive, reverse):
    chunk = lax.broadcasted_iota(jnp.int32, drive.shape, 0)
    for shift in (1, 2, 4):
        if reverse:
            other_decay = pltpu.roll(decay, SUB - shift, 0)
            other_drive = pltpu.roll(drive, SUB - shift, 0)
            inside = chunk < SUB - shift
        else:
            other_decay = pltpu.roll(decay, shift, 0)
            other_drive = pltpu.roll(drive, shift, 0)
            inside = chunk >= shift
        drive = jnp.where(inside, decay * other_drive + drive, drive)
        decay = jnp.where(inside, decay * other_decay, decay)
    return decay, drive


def spread_rows(bcs_ref, spread_ref, bcb):
    bcb[...] = jnp.dot(bcs_ref[...], spread_ref[...], preferred_element_type=F32)


def turn(index, mask, bits):
    for bit in range(bits):
        if mask >> bit & 1:
            index = flip(index, bit)
    return index


class Copies:
    def __init__(self, send_sems, recv_sems):
        self.send_sems, self.recv_sems = send_sems, recv_sems
        self.count, self.open = 0, []

    def remote(self, src, dst, peer):
        k, self.count = self.count, self.count + 1
        copy = pltpu.make_async_remote_copy(
            src_ref=src, dst_ref=dst, send_sem=self.send_sems.at[k],
            recv_sem=self.recv_sems.at[k], device_id=peer, device_id_type=MESH,
        )
        copy.start()
        self.open.append(copy)
        return copy

    def later(self, src_of, dst, peer):
        k, self.count = self.count, self.count + 1

        def make():
            return pltpu.make_async_remote_copy(
                src_ref=src_of(), dst_ref=dst, send_sem=self.send_sems.at[k],
                recv_sem=self.recv_sems.at[k], device_id=peer, device_id_type=MESH,
            )

        self.open.append(make)
        return make

    def local(self, src, dst):
        k, self.count = self.count, self.count + 1
        copy = pltpu.make_async_copy(src, dst, self.send_sems.at[k])
        copy.start()
        return copy

    def drop(self, copy):
        self.open = [other for other in self.open if other is not copy]

    def finish(self):
        for copy in self.open:
            (copy() if callable(copy) else copy).wait_send()


class WtSum:
    def __init__(self, copies, mix, first, half, land, total, seq, wt, bits):
        self.copies, self.mix, self.first, self.total = copies, mix, first, total
        self.half, self.land = half, land
        self.seq, self.wt, self.bits = seq, wt, bits
        size = mix.shape[0] // 2
        mine = bit_of(wt, 0)
        self.kept = pl.ds(pl.multiple_of(mine * size, 16), size)
        self.given = pl.ds(pl.multiple_of((1 - mine) * size, 16), size)

    def begin(self):
        peer = (self.seq, flip(self.wt, 0))
        self.copy = self.copies.remote(self.mix.at[self.given], self.first, peer)

    def so_far(self, bit):
        self.copy.wait_recv()
        if bit == 1:
            return self.mix[self.kept, :] + self.first[...]
        return self.half[bit - 2].astype(F32) + self.land[bit - 2].astype(F32)

    def middle(self, bit):
        self.half[bit - 1] = self.so_far(bit).astype(BF16)
        peer = (self.seq, flip(self.wt, bit))
        self.copy = self.copies.remote(self.half.at[bit - 1], self.land.at[bit - 1], peer)

    def end(self):
        self.end_send()
        self.copy.wait_recv()

    def end_send(self):
        self.total[self.kept, :] = self.so_far(self.bits)
        peer = (self.seq, flip(self.wt, 0))
        part = self.total.at[self.kept]
        self.copy = self.copies.remote(part, part, peer)


def flip(index, bit):
    return index + (1 - 2 * ((index // 2**bit) % 2)) * 2**bit


def bit_of(index, bit):
    return (index // 2**bit) % 2


def pick(left, bit, value):
    return tuple(value if b == bit else slice(None) for b in left)


def over_blocks(count, rows, body):
    tile = math.gcd(rows, 32)
    per_block = rows // tile

    def one(i, carry):
        block, row = i // per_block, (i % per_block) * tile
        index = tuple((block // 2 ** (count - 1 - k)) % 2 for k in range(count))
        body(index, pl.ds(pl.multiple_of(row, tile), tile))
        return carry

    lax.fori_loop(0, 2**count * per_block, one, 0)


class Halving:
    def __init__(self, copies, source, dims, order, columns, landing, final, me, peer):
        self.copies, self.source, self.dims, self.order = copies, source, dims, order
        self.columns, self.landing, self.final = columns, landing, final
        self.mine = {bit: bit_of(me, bit) for bit in order}
        self.theirs = {bit: 1 - value for bit, value in self.mine.items()}
        self.moves = [
            copies.later(functools.partial(self.block, stage), landing[stage], peer(bit))
            for stage, bit in enumerate(order)
        ]

    def left(self, stage):
        return [b for b in self.dims if b not in self.order[:stage]]

    def block(self, stage):
        bit = self.order[stage]
        other = pick(self.left(stage), bit, self.theirs[bit])
        if stage == 0:
            return self.source.at[other + (slice(None), self.columns)]
        return self.landing[stage - 1].at[other]

    def send(self, stage):
        self.moves[stage]().start()

    def add(self, stage):
        self.moves[stage]().wait_recv()
        mine = self.mine[self.order[stage]]
        left, after = self.left(stage), self.left(stage + 1)
        landed = self.landing[stage]

        def body(index, rows):
            at = iter(index)
            full = tuple(mine if b == self.order[stage] else next(at) for b in left)
            if stage == 0:
                kept = self.source[full + (rows, self.columns)]
            else:
                kept = self.landing[stage - 1][full + (rows, slice(None))]
            total = kept.astype(F32) + landed[index + (rows, slice(None))].astype(F32)
            if after:
                landed[index + (rows, slice(None))] = total.astype(BF16)
            else:
                self.final(rows, total)

        over_blocks(len(after), landed.shape[-2], body)


class Group:
    def __init__(self, members, done=None):
        self.members, self.done, self.stage = members, done, 0

    def launch(self):
        for job in self.members:
            job.send(0)

    def act(self, member, stage):
        job = self.members[member]
        if stage:
            job.add(stage - 1)
        if stage < len(job.order):
            job.send(stage)
        else:
            self.stage += 1
            if self.stage == len(self.members) and self.done:
                self.done()

    def advance(self, stage):
        stages = len(self.members[0].order)
        for job in self.members:
            job.add(stage)
            if stage + 1 < stages:
                job.send(stage + 1)
        if stage + 1 == stages and self.done:
            self.done()

    def release(self):
        for job in self.members:
            job.moves[0]().wait_send()
            job.copies.drop(job.moves[0])


def fill(target, at, value):
    rows, lead = target.shape[-2], len(target.shape) - 2
    inner = (value.shape[0] // rows).bit_length() - 1
    index = tuple((at // 2 ** (lead - 1 - k)) % 2 for k in range(lead - inner))
    target[index] = value.reshape((2,) * inner + (rows, value.shape[1])).astype(BF16)


def by_tiles(target, rows, value_of):
    tile = min(512, rows)

    def one(i, carry):
        m = pl.multiple_of(i * tile, tile)
        fill(target, i * (tile // target.shape[-2]), value_of(pl.ds(m, tile)))
        return carry

    lax.fori_loop(0, rows // tile, one, 0)


def seq_orders(width, seq_bits, low=None):
    low = width - LANE if low is None else low
    first = tuple(range(seq_bits))
    orders = ((0, low, first), (low, width - low, (1, 0) + first[2:]))
    return [item for item in orders if item[1]]


def timetable(groups, loads=()):
    rate, delay, turn_time, ahead = 23.3, 4.0, 1.0, 8.0
    jobs, free, clock, found = [], {}, 0.0, []
    for g, (ready, axis, size, members) in enumerate(groups):
        for m, (columns, order) in enumerate(members):
            jobs.append([ready, ready, g, m, 0, columns * size, axis, order])
    for ready, axis, bit, size in loads:
        jobs.append([ready, ready, -1, 0, 0, 2 * size, axis, (bit,)])
    while jobs:
        best = None
        for job in jobs:
            ready, made, g, m, stage, size, axis, order = job
            issue = max(clock, ready)
            if stage < len(order):
                bit = order[stage]
                link = (axis, min(bit, 1))
                issue = max(issue, free.get(link, 0.0) - ahead)
            key = (issue, -stage, made, g, m)
            if best is None or key < best[0]:
                best = (key, job)
        (issue, *_), job = best
        ready, made, g, m, stage, size, axis, order = job
        if g >= 0:
            found.append((issue, g, m, stage))
        clock = issue + (turn_time if stage else 0.1)
        if stage == len(order):
            jobs.remove(job)
            continue
        bit = order[stage]
        link = (axis, min(bit, 1))
        took = size / 2 ** (stage + 1) * rate
        if axis == "wt" and bit == 0:
            took = took / 6
        start = max(clock, free.get(link, 0.0))
        free[link] = end = start + took
        if bit > 1:
            start = max(start, free.get((axis, bit), 0.0))
            free[axis, bit] = end = start + 2 * took
        job[0], job[4] = end + delay, stage + 1
    return found


def seq_group(copies, source, name, take, final, seq, peer, done=None, low=None):
    seq_bits = len(source.shape) - 2
    dims = list(reversed(range(seq_bits)))
    if name == "chan":
        dims = [0] + dims[:-1]
    members = []
    for start, size, order in seq_orders(source.shape[-1], seq_bits, low):
        members.append(
            Halving(
                copies, source, dims, order, slice(start, start + size), take(seq_bits),
                functools.partial(final, start), seq, peer,
            )
        )
    return Group(members, done)


def landings(bits, rows, widths):
    return [
        pltpu.VMEM((2,) * (bits - 1 - stage) + (rows, width), BF16)
        for width in widths
        for stage in range(bits)
    ]


def seq_landings(seq_bits, rows, widths, low=None):
    found = []
    for width in widths:
        sizes = [size for _, size, _ in seq_orders(width, seq_bits, low)]
        found += landings(seq_bits, rows, sizes)
    return found


def wout_lows(n_wide, late):
    return [WIDE // 2 if late else 3 * WIDE // 4] + [7 * WIDE // 8 if late else WIDE // 2] * (n_wide - 1)


def feat_plan(n_chan, parts):
    half = n_chan // 2
    plan = [
        (n_chan + half, half, 3 * half // 4), (0, half, half), (half, half // 2, half // 2),
        (half + half // 2, half // 2, half // 4),
    ]
    return plan if parts > 1 else [(n_chan, half, None)] + plan


def feat_type(n_feat, n_seq, n_wt):
    return BF16 if n_feat // (n_seq * n_wt) % 16 == 0 else F32


def parts_of(n_chan, n_seq):
    return 2 if n_chan // n_seq >= 32 else 1


WIDE = 1024
EARLY = 512


def join_rounds(
    n_seq, n_streams, seq, wt, rate, head_ref, tail_ref, run_s, span_in, span_s, gap_s, send_s,
    land_s, span_send, span_land, send_sems, recv_sems,
):
    head_ref[...] = jnp.zeros_like(head_ref)
    tail_ref[...] = jnp.zeros_like(tail_ref)
    gap_s[...] = jnp.zeros_like(gap_s)
    for k in range(2 * n_streams):
        span_s[k : k + 1, :] = span_in[k % n_streams]
    started = []
    for r in range(n_seq.bit_length() - 1):
        d = 2**r
        if r > 1:
            for inside, copies in started[2 * r - 4 : 2 * r - 2]:

                @pl.when(inside)
                def _():
                    copies[0].wait_send()

        send_s[r % 2] = run_s[...].astype(BF16)
        span_send[r] = span_s[...]
        up = (seq + d < n_seq, lax.rem(seq + d, n_seq))
        down = (seq >= d, lax.rem(seq + n_seq - d, n_seq))
        for way, (inside, other) in enumerate((up, down)):
            copies = [
                pltpu.make_async_remote_copy(
                    src_ref=src, dst_ref=dst, send_sem=send_sems.at[r, way, k],
                    recv_sem=recv_sems.at[r, way, k], device_id=(other, wt), device_id_type=MESH,
                )
                for k, (src, dst) in enumerate(
                    ((send_s.at[r % 2, way], land_s.at[r, way]), (span_send.at[r], span_land.at[r, way]))
                )
            ]

            @pl.when(inside)
            def _():
                for copy in copies:
                    copy.start()

            started.append((inside, copies))
        for way, inside in ((0, down[0]), (1, up[0])):
            copies = started[-2 + way][1]
            out = (head_ref, tail_ref)[way]

            @pl.when(inside)
            def _():
                for copy in copies:
                    copy.wait_recv()
                for b in range(n_streams):
                    k = way * n_streams + b
                    landed = land_s[r, way, b].astype(F32)
                    span = span_land[r, way, k : k + 1, :]
                    gap, own = gap_s[k : k + 1, :], span_s[k : k + 1, :]
                    out[b] = out[b] + jnp.exp2(rate * gap) * landed
                    run_s[way, b] = run_s[way, b] + jnp.exp2(rate * own) * landed
                    gap_s[k : k + 1, :] = gap + span
                    span_s[k : k + 1, :] = own + span

    for at, (inside, copies) in enumerate(started):

        @pl.when(inside)
        def _():
            for copy in copies[at < len(started) - 4 :]:
                copy.wait_send()


def early_sums(n_seq, part, stream, width, grad_ref, normed_t_ref, wout_ref, feat_ref, scratch):
    gated_s, dgate_s, grads, normed_t = scratch[:4]
    feat_parts, scratch = scratch[4:6], scratch[6:]
    seq_bits = n_seq.bit_length() - 1
    count = grads.shape[1] // WIDE
    wout_parts, scratch = scratch[:count], scratch[count:]
    load_sems, send_sems, recv_sems = scratch[:3]
    scratch = scratch[3:]
    take = lambda k: [scratch.pop(0) for _ in range(k)]
    seq, wt = lax.axis_index("seq"), lax.axis_index("wt")
    copies = Copies(send_sems, recv_sems)
    peer = lambda bit: (flip(seq, bit), wt)

    def loads():
        return [
            pltpu.make_async_copy(grad_ref, grads, load_sems.at[0]),
            pltpu.make_async_copy(normed_t_ref, normed_t, load_sems.at[1]),
        ]

    def wout_final(at, start, rows, total):
        wout_ref[rows, at + start : at + start + total.shape[1]] = total.astype(BF16)

    def feat_final(at, start, rows, total):
        columns = slice(at + start, at + start + total.shape[1])
        feat_ref[rows, columns] = total.astype(feat_ref.dtype)

    lows = wout_lows(count, False)
    wouts = [
        seq_group(
            copies, wout_parts[k], "chan", take, functools.partial(wout_final, k * WIDE), seq, peer,
            low=lows[k],
        )
        for k in range(count)
    ]
    width = EARLY // 2
    feats = [
        seq_group(
            copies, feat_parts[k], "feat", take, functools.partial(feat_final, k * width), seq, peer
        )
        for k in range(2)
    ]
    groups = wouts + feats

    @pl.when((part == 0) & (stream == 0))
    def _():
        barrier = pltpu.get_barrier_semaphore()
        for bit in range(seq_bits):
            pl.semaphore_signal(barrier, inc=1, device_id=peer(bit), device_id_type=MESH)
        pl.semaphore_wait(barrier, seq_bits)
        for copy in loads():
            copy.start()

    def begin():
        for copy in loads():
            copy.wait()
        for k in range(count):
            for inner in range(0, WIDE, 512):
                at = k * WIDE + inner
                value = jnp.dot(
                    gated_s[...], grads[:, at : at + 512], preferred_element_type=F32
                )
                rows, lead = wout_parts[k].shape[-2], len(wout_parts[k].shape) - 2
                wout_parts[k][(slice(None),) * (lead + 1) + (slice(inner, inner + 512),)] = (
                    value.reshape((2,) * lead + (rows, 512)).astype(BF16)
                )

    def begin_feat():
        for k in range(2):
            at = slice(k * width, (k + 1) * width)
            by_tiles(
                feat_parts[k], normed_t.shape[0],
                lambda m: jnp.dot(normed_t[m, :], dgate_s[:, at], preferred_element_type=F32),
            )

    entries = []
    for which, group in enumerate(groups):
        rows = math.prod(group.members[0].source.shape[:-1])
        members = [(one.columns.stop - one.columns.start, one.order) for one in group.members]
        ready = 2.0 if which < count else 8.0
        entries.append((ready, "seq", rows * 2 / 2**20, members))
    times = [3.5, 9.0] + [9.0 + 2.9 * k for k in range(1, 15)]
    moments, last = {}, []
    for at, which, member, stage in timetable(entries):
        turns = [k for k, time in enumerate(times) if time >= at]
        moments.setdefault(turns[0] if turns else 16, []).append((which, member, stage))

    def moment(turn):
        if turn < 2:

            @pl.when((part == 1) & (stream == 0))
            def _():
                (begin, begin_feat)[turn]()

        for at in range(4):
            if at * 4 + turn in moments:

                @pl.when((part == 1) & (stream == at))
                def _():
                    for which, member, stage in moments[at * 4 + turn]:
                        groups[which].act(member, stage)

    def rest():
        for which, member, stage in moments.get(16, []):
            groups[which].act(member, stage)
        copies.finish()

    return moment, rest


def scan_kernel(
    n_state, n_seq, parts, bcs_ref, spread_ref, gather_ref, raw_ref, u_ref, g_ref, gate_ref, dgated_ref,
    bias_ref, skip_ref, a_ref, end_ref, lead_ref, total_ref, head_ref, tail_ref, grad_ref,
    normed_t_ref,
    gated_ref, gated_t_ref, dgate_ref, dscan_ref, draw_ref, dbc_ref, da_ref, sums_ref, wout_ref,
    feat_ref,
    bcb, acc_all, dec_in, delta_in, drive_in, g_in, y_sum, b_sum, d_sum, kept, decays, da_sum, row_sum, *scratch,
):
    n_rows, width = raw_ref.shape
    steps = n_rows // SUB
    part, stream = pl.program_id(0), pl.program_id(1)
    n_streams = pl.num_programs(1)
    acc = acc_all.at[stream]
    if parts > 1:
        early_moment, early_rest = early_sums(
            n_seq, part, stream, width, grad_ref, normed_t_ref, wout_ref, feat_ref, list(scratch)
        )
    start_at = 2 * n_state * LANE
    columns = pl.ds(pl.multiple_of(part * width, width), width)
    spread_rows(bcs_ref, spread_ref, bcb)

    @pl.when(part == 0)
    def _():
        acc_all[stream] = jnp.zeros(acc_all.shape[1:], F32)

    @pl.when(stream == 0)
    def _():
        da_sum[...] = jnp.zeros_like(da_sum)
        row_sum[...] = jnp.zeros_like(row_sum)

    def prepare(j, carry):
        rows = pl.ds(pl.multiple_of(j * 16, 16), 16)
        delta = softplus(raw_ref[rows, :].astype(F32) + bias_ref[...])
        starts = wide(bcb[rows, start_at : start_at + LANE], width)
        delta_in[rows, :] = delta
        dec_in[rows, :] = jnp.where(starts > 0.5, RESET, delta)
        drive_in[rows, :] = delta * u_ref[rows, :].astype(F32)
        g_in[rows, :] = g_ref[rows, :].astype(F32)
        return carry

    lax.fori_loop(0, steps // 2, prepare, 0)
    chunk = lax.broadcasted_iota(jnp.int32, (SUB, width), 0)
    total = total_ref[0]
    before, after = total, total
    for shift in (1, 2, 4):
        before = jnp.where(chunk >= shift, before + pltpu.roll(before, shift, 0), before)
        after = jnp.where(chunk < SUB - shift, after + pltpu.roll(after, SUB - shift, 0), after)
    before, after = pltpu.roll(before, 1, 0), pltpu.roll(after, SUB - 1, 0)

    for first in range(0, n_state, NBLK):
        if parts > 1:
            early_moment(first // NBLK)
        states = range(first, first + NBLK)
        entry, incoming = [], []
        for n in states:
            head, tail = head_ref[0, n : n + 1, :], tail_ref[0, n : n + 1, :]
            inner = pltpu.roll(end_ref[0, n], 1, 0) + jnp.exp2(before * a_ref[n : n + 1, :]) * head
            outer = pltpu.roll(lead_ref[0, n], SUB - 1, 0) + jnp.exp2(after * a_ref[n : n + 1, :]) * tail
            entry.append(jnp.where(chunk == 0, head, inner))
            incoming.append(jnp.where(chunk == SUB - 1, tail, outer))

        def forward(j, carry):
            rows = pl.ds(pl.multiple_of(j * SUB, SUB), SUB)
            held, drive, g = dec_in[rows, :], drive_in[rows, :], g_in[rows, :]
            running = []
            y = y_sum[rows, :] if first else None
            for k, (n, h) in enumerate(zip(states, carry)):
                b = wide(bcb[rows, n * LANE : (n + 1) * LANE], width)
                c_at = slice((n_state + n) * LANE, (n_state + n + 1) * LANE)
                c = wide(bcb[rows, c_at], width)
                decay = jnp.exp2(held * a_ref[n : n + 1, :])
                kept[k, rows, :] = h
                decays[k, rows, :] = decay
                h = decay * h + drive * b
                y = c * h if y is None else y + c * h
                acc[rows, c_at] += fold(h * g)
                running.append(h)
            y_sum[rows, :] = y
            return tuple(running)

        lax.fori_loop(0, steps, forward, tuple(entry), unroll=8)

        def backward(j, carry):
            rows = pl.ds(pl.multiple_of((steps - 1 - j) * SUB, SUB), SUB)
            delta, drive, g = delta_in[rows, :], drive_in[rows, :], g_in[rows, :]
            through = b_sum[rows, :] if first else None
            pulled = d_sum[rows, :] if first else None
            passed, da = [], []
            for k, (n, p, da_n) in enumerate(zip(states, carry[0], carry[1])):
                b_at = slice(n * LANE, (n + 1) * LANE)
                b = wide(bcb[rows, b_at], width)
                c = wide(bcb[rows, (n_state + n) * LANE : (n_state + n + 1) * LANE], width)
                adjoint = g * c + p
                p = decays[k, rows, :] * adjoint
                weighed = p * kept[k, rows, :]
                pulled = weighed * a_ref[n : n + 1, :] if pulled is None else pulled + weighed * a_ref[n : n + 1, :]
                through = adjoint * b if through is None else through + adjoint * b
                acc[rows, b_at] += fold(adjoint * drive)
                passed.append(p)
                da.append(da_n + weighed * delta)
            b_sum[rows, :] = through
            d_sum[rows, :] = pulled
            return tuple(passed), tuple(da)

        zero = tuple(jnp.zeros((SUB, width), F32) for _ in states)
        _, da = lax.fori_loop(0, steps, backward, (tuple(incoming), zero), unroll=8)
        for n, da_n in zip(states, da):
            da_sum[n] += da_n

    def finish(j, carry):
        bias_sum, skip_sum = carry
        rows = pl.ds(pl.multiple_of(j * 16, 16), 16)
        u, g, delta = u_ref[rows, :].astype(F32), g_in[rows, :], delta_in[rows, :]
        gate, d_gated = gate_ref[rows, :].astype(F32), dgated_ref[rows, :]
        scanned = (y_sum[rows, :] + skip_ref[...] * u).astype(BF16).astype(F32)
        sig = jax.nn.sigmoid(gate)
        gated_ref[rows, :] = (scanned * gate * sig).astype(BF16)
        d_gate = d_gated * scanned * sig * (1.0 + gate * (1.0 - sig))
        dgate_ref[rows, :] = d_gate.astype(BF16)
        through = b_sum[rows, :]
        dscan_ref[rows, :] = (delta * through + skip_ref[...] * g).astype(BF16)
        slope = jax.nn.sigmoid(raw_ref[rows, :].astype(F32) + bias_ref[...])
        d_pre = (d_sum[rows, :] * (1.0 / LOG2E) + u * through) * slope
        draw_ref[rows, :] = d_pre.astype(BF16)
        gu = g * u
        return bias_sum + d_pre[:SUB] + d_pre[SUB:], skip_sum + gu[:SUB] + gu[SUB:]

    zero = jnp.zeros((SUB, width), F32)
    bias_sum, skip_sum = lax.fori_loop(0, steps // 2, finish, (zero, zero))
    gated_t_ref[...] = gated_ref[...].T
    if parts > 1:
        gated_s, dgate_s = scratch[:2]

        @pl.when(part == 0)
        def _():
            at = pl.ds(pl.multiple_of(stream * n_rows, n_rows), n_rows)
            gated_s[:, at] = gated_t_ref[...]
            dgate_s[at, :] = dgate_ref[...]

    row_sum[0] += bias_sum
    row_sum[1] += skip_sum

    @pl.when(stream == n_streams - 1)
    def _():
        for n in range(n_state):
            da_ref[n : n + 1, columns] = jnp.sum(da_sum[n], 0, keepdims=True)
        for k in range(2):
            sums_ref[k : k + 1, columns] = jnp.sum(row_sum[k], 0, keepdims=True)


    last = part == pl.num_programs(0) - 1

    @pl.when(last)
    def _():
        found = jnp.dot(
            acc[...], gather_ref[...], precision=lax.Precision.HIGHEST, preferred_element_type=F32
        )

        @pl.when(stream == 0)
        def _():
            dbc_ref[...] = found

        @pl.when(stream > 0)
        def _():
            dbc_ref[...] += pltpu.roll(found, stream * 2 * n_state, 1)

    if parts > 1:

        @pl.when(last & (stream == n_streams - 1))
        def _():
            early_rest()


def spread_matrix(n_state):
    count = 2 * n_state + 1
    column = np.arange(count * LANE)[None, :] // LANE
    return jnp.asarray((np.arange(LANE)[:, None] == column).astype(ml_dtypes.bfloat16))


def gather_matrix(n_state):
    row = np.arange(2 * n_state * LANE)[:, None] // LANE
    return jnp.asarray((np.arange(LANE)[None, :] == row).astype(np.float32))


def scan_specs(n_streams, n_rows, n_chan, n_state, width):
    row = pl.BlockSpec((n_rows, width), lambda b, c: (b, c))
    thin = pl.BlockSpec((n_rows, LANE), lambda b, c: (b, 0))
    chan = pl.BlockSpec((1, width), lambda b, c: (0, c))
    rate = pl.BlockSpec((n_state, width), lambda b, c: (0, c))
    edge = pl.BlockSpec((1, n_state, SUB, width), lambda b, c: (b, 0, 0, c))
    total = pl.BlockSpec((1, SUB, width), lambda b, c: (b, 0, c))
    head = pl.BlockSpec((1, n_state, width), lambda b, c: (b, 0, c))
    return row, thin, chan, rate, edge, total, head


def whole(shape):
    return pl.BlockSpec(shape, lambda b, c: (0,) * len(shape))


def scan_all(
    bcs, raw, u, g, gate, d_gated, bias, skip, rates, ends, leads, totals, heads, tails, grads,
    normed_t,
):
    n_seq, n_streams = lax.axis_size("seq"), lax.axis_size("wt")
    n_rows, n_chan = raw.shape[0] // n_streams, raw.shape[1]
    n_state, n_feat = rates.shape[0], normed_t.shape[0]
    width = min(512, n_chan)
    parts = parts_of(n_chan, n_seq)
    seq_bits = n_seq.bit_length() - 1

    def swapped(spec):
        return pl.BlockSpec(spec.block_shape, lambda c, b: spec.index_map(b, c))

    row, thin, chan, rate, edge, total, head = map(
        swapped, scan_specs(n_streams, n_rows, n_chan, n_state, width)
    )
    count = (2 * n_state + 1) * LANE
    spread = spread_matrix(n_state)
    gather = gather_matrix(n_state)
    rows = jax.ShapeDtypeStruct(raw.shape, BF16)
    hbm = pl.BlockSpec(memory_space=pl.ANY)
    wout_rows, feat_rows = max(n_chan // parts // n_seq, 16), n_feat // n_seq
    scratch = [
        pltpu.VMEM((n_rows, count), F32),
        pltpu.VMEM((n_streams, n_rows, 2 * n_state * LANE), F32),
    ]
    scratch += [pltpu.VMEM((n_rows, width), F32)] * 7
    scratch += [pltpu.VMEM((NBLK, n_rows, width), F32)] * 2
    scratch += [pltpu.VMEM((n_state, SUB, width), F32), pltpu.VMEM((2, SUB, width), F32)]
    params = {}
    if parts > 1:
        blocks = (2,) * seq_bits
        n_wide = n_feat // WIDE
        scratch += [
            pltpu.VMEM((width, raw.shape[0]), BF16),
            pltpu.VMEM((raw.shape[0], width), BF16),
            pltpu.VMEM((raw.shape[0], n_feat), BF16),
            pltpu.VMEM(normed_t.shape, BF16),
        ]
        scratch += [pltpu.VMEM(blocks + (feat_rows, EARLY // 2), BF16)] * 2
        scratch += [pltpu.VMEM(blocks + (wout_rows, WIDE), BF16)] * n_wide
        scratch += [pltpu.SemaphoreType.DMA((2,))]
        scratch += [pltpu.SemaphoreType.DMA((2 * seq_bits * (n_wide + 2),))] * 2
        for low in wout_lows(n_wide, False):
            scratch += seq_landings(seq_bits, wout_rows, [WIDE], low)
        scratch += seq_landings(seq_bits, feat_rows, [EARLY // 2] * 2)
        params = dict(collective_id=4, has_side_effects=True)
    return pl.pallas_call(
        functools.partial(scan_kernel, n_state, n_seq, parts),
        grid=(n_chan // width, n_streams),
        in_specs=[
            thin, whole((LANE, count)), whole(gather.shape), row, row, row, row, row,
            chan, chan, rate, edge, edge, total, head, head, hbm, hbm,
        ],
        out_specs=[
            row, pl.BlockSpec((width, n_rows), lambda c, b: (c, b)), row, row, row,
            whole((n_rows, LANE)), whole((n_state, n_chan)), whole((2, n_chan)),
            whole((wout_rows, n_feat)), whole((feat_rows, EARLY)),
        ],
        out_shape=[
            rows, jax.ShapeDtypeStruct(raw.shape[::-1], BF16), rows, rows, rows,
            jax.ShapeDtypeStruct((n_rows, LANE), F32),
            jax.ShapeDtypeStruct((n_state, n_chan), F32),
            jax.ShapeDtypeStruct((2, n_chan), F32),
            jax.ShapeDtypeStruct((wout_rows, n_feat), BF16),
            jax.ShapeDtypeStruct((feat_rows, EARLY), feat_type(n_feat, n_seq, n_streams)),
        ],
        scratch_shapes=scratch,
        compiler_params=pltpu.CompilerParams(vmem_limit_bytes=63 * 2**20, **params),
        name="scan_all",
    )(
        bcs, spread, gather, raw, u, g, gate, d_gated, bias, skip, rates,
        ends, leads, totals, heads, tails, grads, normed_t,
    )


def finish_kernel(
    n_seq, n_wt, n_state,
    gated_t_ref, dgate_ref, dscan_ref, draw_ref, u_ref, conv_ref, grad_ref, normed_t_ref, win_ref,
    wout_ref, feat_ref, gated_ref, w_out_ref, x_ref, g_ref,
    gain_ref, dbc_ref, low_ref, wx_ref, wdt_ref, wconv_ref, bconv_ref, da_ref, a_ref, sums_ref,
    feat_out, wout_out, small_out, norm_out, out_out, gain_out,
    *scratch,
):
    scratch = list(scratch)
    take = lambda count: [scratch.pop(0) for _ in range(count)]
    seq, wt = lax.axis_index("seq"), lax.axis_index("wt")
    seq_bits, wt_bits = n_seq.bit_length() - 1, n_wt.bit_length() - 1
    seq_peer = lambda bit: (flip(seq, bit), wt)
    wt_peer = lambda bit: (seq, flip(wt, bit))
    n_chan, all_rows = gated_t_ref.shape
    parts = parts_of(n_chan, n_seq)
    ready = parts - 1
    half_seq = n_seq // 2
    here = n_wt * seq + wt
    mine = (seq % 2) * half_seq + seq // 2

    def summed_at(j):
        return (j % half_seq) * 2 + j // half_seq

    def device(flat):
        return flat // n_wt, flat % n_wt

    flat = n_seq * wt + mine
    owner, giver_block = device(flat), here % n_seq
    giver = (summed_at(giver_block), here // n_seq)
    elsewhere = flat != here
    per = n_seq // parts
    part_flat = [n_seq * wt + q * per + mine // parts for q in range(parts)]
    part_owner = [device(value) for value in part_flat]
    piece = mine % parts
    piece_giver = [
        (summed_at((giver_block % per) * parts + k), here // n_seq) for k in range(parts)
    ]
    piece_here = [n_wt * s + w == here for s, w in piece_giver]
    ahead, behind = (lax.rem(seq + 1, n_seq), wt), (lax.rem(seq + n_seq - 1, n_seq), wt)

    barrier = pltpu.get_barrier_semaphore()
    partners = [seq_peer(b) for b in range(seq_bits)]
    partners += [(seq, turn(wt, mask, wt_bits)) for mask in range(1, n_wt)]
    partners += [ahead, behind]
    for partner in partners:
        pl.semaphore_signal(barrier, inc=1, device_id=partner, device_id_type=MESH)

    arrivals = len(partners) + 2 * elsewhere.astype(jnp.int32)

    @pl.when(elsewhere)
    def _():
        for partner in (owner, giver):
            pl.semaphore_signal(barrier, inc=1, device_id=partner, device_id_type=MESH)

    if parts > 1:
        others = [(value != here, to) for value, to in zip(part_flat, part_owner)]
        others += [(jnp.logical_not(own), to) for own, to in zip(piece_here, piece_giver)]
        for away, to in others:
            arrivals = arrivals + away.astype(jnp.int32)

            @pl.when(away)
            def _():
                pl.semaphore_signal(barrier, inc=1, device_id=to, device_id_type=MESH)

    (
        gated_t, dgate, dscan, draw, normed_t, grads, win_rows, conv, d_conv, mix, first, half, land, fin,
        u_all, ddt, dbc, pack, rim_f, rim_s, fin_feat, fin_wout, fin_small, w_rows, gain_sum, small,
        piece_sems, send_sems, recv_sems,
    ) = take(29)
    n_wide = normed_t.shape[0] // WIDE
    wout_parts = take(n_wide) if ready else take(1) * n_wide
    feat_parts, norm_parts = take(4 if ready else 3), take(2)
    if not ready:
        inner = (slice(None),) * (seq_bits + 1)
        feat_parts += [feat_parts[0].at[inner + (slice(at, at + 256),)] for at in (0, 256)]
    copies = Copies(send_sems, recv_sems)
    part_chan = gated_t.shape[0]
    if not ready:
        u_all = gated_t
    n_feat = normed_t.shape[0]
    n_rows = all_rows // n_wt
    taps = wconv_ref.shape[0]
    steps = n_rows // SUB
    rim = (taps - 1) * SUB
    cols = 512

    def load(src, dst):
        return copies.local(src, dst)

    def grad_block(k):
        return load(grad_ref.at[:, :, k * cols : (k + 1) * cols], grads.at[k % 2])

    coming = {
        "draw": load(draw_ref, draw),
        "gated": load(gated_t_ref.at[ready * part_chan :], gated_t),
        0: grad_block(0),
        1: grad_block(1),
        "normed": load(normed_t_ref, normed_t),
        "dgate": load(dgate_ref, dgate),
        "conv": load(conv_ref.at[:, :, :cols], conv),
        "dscan": load(dscan_ref.at[:, :cols], dscan),
        "w_rows": load(
            win_ref.at[pl.ds(pl.multiple_of(seq * w_rows.shape[0], 16), w_rows.shape[0])], w_rows
        ),
    }

    ring, d_block = win_rows.shape[:2]

    def win_block(i):
        coming["win", i] = load(win_ref.at[i * d_block : (i + 1) * d_block], win_rows.at[i % ring])

    for k in range(cols // d_block):
        win_block(k)
    if ready:
        coming["wout"] = load(wout_ref, fin_wout.at[0])
        coming["feat"] = load(feat_ref, fin_feat.at[:, n_chan : n_chan + EARLY])
    pl.semaphore_wait(barrier, arrivals)

    rows_own = feat_out.shape[0]

    def own_rows(w):
        return pl.ds(pl.multiple_of(w * rows_own, 8), rows_own)

    delivered = []

    def to_wt(block_of, place):
        for mask in range(1, n_wt):
            peer = turn(wt, mask, wt_bits)
            delivered.append(copies.remote(block_of(peer), place, (seq, peer)).wait_recv)
        delivered.append(copies.local(block_of(wt), place).wait)

    def feat_done(at, cols):
        tile = math.gcd(w_rows.shape[0], 32)

        def body(i, carry):
            rows = pl.ds(pl.multiple_of(i * tile, tile), tile)
            done = fin_feat[rows, at : at + cols].astype(F32)
            product = w_rows[rows, at : at + cols].astype(F32) * done
            gain_sum[rows, :] += fold(product)
            return carry

        lax.fori_loop(0, w_rows.shape[0] // tile, body, 0)
        start = pl.multiple_of(((at // n_chan) * n_wt + wt) * n_chan + at % n_chan, LANE)
        to_wt(
            lambda w: fin_feat.at[own_rows(w), at : at + cols],
            feat_out.at[:, pl.ds(start, cols)],
        )

    moved = []

    def small_done():
        k, copies.count = copies.count, copies.count + 1
        away = pltpu.make_async_remote_copy(
            src_ref=fin_small, dst_ref=small_out, send_sem=send_sems.at[k],
            recv_sem=recv_sems.at[k], device_id=owner, device_id_type=MESH,
        )
        home = pltpu.make_async_copy(fin_small, small_out, send_sems.at[k])

        @pl.when(elsewhere)
        def _():
            away.start()

        @pl.when(jnp.logical_not(elsewhere))
        def _():
            home.start()

        def wait():
            @pl.when(elsewhere)
            def _():
                away.wait()

            @pl.when(jnp.logical_not(elsewhere))
            def _():
                home.wait()

        moved.append(wait)

    def wout_done(q, at, width, slot):
        place = fin_wout.at[q, :, at : at + width]
        target = wout_out.at[piece, :, at : at + width]
        away = pltpu.make_async_remote_copy(
            src_ref=place, dst_ref=target, send_sem=piece_sems.at[0, q, slot],
            recv_sem=piece_sems.at[1, piece, slot], device_id=part_owner[q], device_id_type=MESH,
        )
        home = pltpu.make_async_copy(place, target, piece_sems.at[0, q, slot])
        remote = part_flat[q] != here

        @pl.when(remote)
        def _():
            away.start()

        @pl.when(jnp.logical_not(remote))
        def _():
            home.start()

        def wait():
            @pl.when(remote)
            def _():
                away.wait_send()

            @pl.when(jnp.logical_not(remote))
            def _():
                home.wait()

        moved.append(wait)

    def wout_arrive(k, at, width, slot):
        target = wout_out.at[k, :, at : at + width]
        copy = pltpu.make_async_remote_copy(
            src_ref=target, dst_ref=target, send_sem=piece_sems.at[0, k, slot],
            recv_sem=piece_sems.at[1, k, slot], device_id=piece_giver[k], device_id_type=MESH,
        )

        @pl.when(jnp.logical_not(piece_here[k]))
        def _():
            copy.wait_recv()

    def wout_final(at, start, rows, total):
        columns = slice(at + start, at + start + total.shape[1])
        fin_wout[ready, rows, columns] = total.astype(BF16)

    def feat_final(at, start, rows, total):
        columns = slice(at + start, at + start + total.shape[1])
        fin_feat[rows, columns] = total.astype(fin_feat.dtype)

    def small_final(start, rows, total):
        fin_small[rows, start : start + total.shape[1]] = total.astype(BF16)

    wout_groups = [
        seq_group(
            copies, wout_parts[k], "chan", take, functools.partial(wout_final, k * WIDE), seq,
            seq_peer, functools.partial(wout_done, ready, k * WIDE, WIDE, k), lows[k],
        )
        for k, lows in zip(range(n_wide), [wout_lows(n_wide, True)] * n_wide)
    ]
    feat_groups = []
    for part, (at, _, low) in zip(feat_parts, feat_plan(n_chan, parts)):
        done = functools.partial(feat_done, at, part.shape[-1])
        feat_groups.append(
            seq_group(
                copies, part, "feat", take, functools.partial(feat_final, at), seq, seq_peer, done,
                low,
            )
        )
    gate_a, gate_b, conv_a, conv_b, conv_c = range(-ready, 5 - ready)
    small_group = seq_group(copies, small, "chan", take, small_final, seq, seq_peer, small_done)
    wide_groups = []
    for target in (norm_out, out_out):
        for k in range(n_feat // cols):

            def final(rows, total, target=target, k=k):
                target[rows, k * cols : (k + 1) * cols] = total

            order = tuple(range(wt_bits))
            job = Halving(
                copies, norm_parts[k % 2], list(reversed(order)), order, slice(0, cols),
                take(wt_bits), final, wt, wt_peer,
            )
            wide_groups.append(Group([job]))

    def wout(k):
        if not ready and k:
            take_until(k - 1)
            wout_groups[k - 1].release()
        for inner in range(WIDE // cols):
            block = k * (WIDE // cols) + inner
            coming[block].wait()
            right = grads[block % 2].reshape(all_rows, cols)
            lanes = slice(inner * cols, (inner + 1) * cols)
            tile = min(512, part_chan)
            rows, lead = wout_parts[k].shape[-2], len(wout_parts[k].shape) - 2
            within = (tile // rows).bit_length() - 1
            for m in range(0, part_chan, tile):
                value = jnp.dot(gated_t[m : m + tile, :], right, preferred_element_type=F32)
                index = tuple(
                    (m // rows >> (lead - 1 - q)) & 1 for q in range(lead - within)
                )
                wout_parts[k][index + (slice(None),) * (within + 1) + (lanes,)] = (
                    value.reshape((2,) * within + (rows, cols)).astype(BF16)
                )
            if block + 2 < n_feat // cols:
                coming[block + 2] = grad_block(block + 2)

    gain_sum[...] = jnp.zeros_like(gain_sum)
    coming["draw"].wait()
    for b in range(n_wt):
        at = slice(b * n_rows, (b + 1) * n_rows)
        mix[at, :] = jnp.dot(draw[at, :], wdt_ref[...], preferred_element_type=F32)
    width = LANE // n_wt
    mix[all_rows:, :] = dbc_ref[...]
    mixed = WtSum(copies, mix, first, half, land, fin, seq, wt, wt_bits)
    mixed.begin()
    coming["gated"].wait()

    def feat(k, right):
        if not ready and k == conv_b:
            take_until(first_feat + gate_a)
            feat_groups[gate_a].release()
        by_tiles(
            feat_parts[k], n_feat,
            lambda m: jnp.dot(normed_t[m, :], right, preferred_element_type=F32),
        )

    def low_pack():
        pack[LANE : 2 * LANE, :] = lax.dot_general(
            low_ref[...], draw[...], (((0,), (0,)), ((), ())), preferred_element_type=F32
        )
        mixed.end_send()
        coming["normed"].wait()
        coming["dgate"].wait()

    def early_feat():
        coming["w_rows"].wait()
        if ready:
            coming["feat"].wait()
            feat_done(n_chan, EARLY)
        mixed.copy.wait_recv()
        mixed_ready()

    tail_at = 2 * LANE + 3 * n_state

    def mixed_ready():
        ddt[...] = fin[:all_rows, :].astype(BF16)
        lane = lax.broadcasted_iota(jnp.int32, (n_rows, LANE), 1)
        for b in range(n_wt):
            part = fin[all_rows:, :]
            if b:
                part = pltpu.roll(part, LANE - b * width, 1)
            dbc[b * n_rows : (b + 1) * n_rows, :] = jnp.where(lane < width, part, 0.0).astype(BF16)
        coming["u"] = load(u_ref, u_all)

        pack[2 * LANE :, :] = jnp.zeros((LANE, n_chan), F32)
        pack[tail_at - n_state : tail_at, :] = da_ref[...] * (a_ref[...] * (1.0 / LOG2E))
        pack[tail_at + taps + 1 : tail_at + taps + 3, :] = sums_ref[...]

    def sums_of(total):
        return jnp.sum(total, 0, keepdims=True)

    chunk = lax.broadcasted_iota(jnp.int32, (SUB, cols), 0)
    rim_moves = []

    def conv_first(h):
        at = slice(h * cols, (h + 1) * cols)
        for b in range(n_wt):
            rows = slice(b * n_rows, (b + 1) * n_rows)
            d_in = lax.dot_general(
                ddt[rows, :], wx_ref[at, :LANE], (((1,), (1,)), ((), ())), preferred_element_type=F32
            )
            d_in = d_in + lax.dot_general(
                dbc[rows, : 2 * n_state], wx_ref[at, LANE:], (((1,), (1,)), ((), ())),
                preferred_element_type=F32,
            )
            d_conv[h, b, :n_rows, :] = d_in
        coming["conv"].wait()
        coming["dscan"].wait()

        def one(i, carry):
            b, j = i // (n_rows // 16), i % (n_rows // 16)
            rows = pl.ds(pl.multiple_of(j * 16, 16), 16)
            taken = [
                conv[b, pl.ds(pl.multiple_of(j * 16 + k * SUB, SUB), 16), :] for k in range(taps)
            ]
            out = bconv_ref[:, at]
            for k in range(taps):
                out = out + taken[k] * wconv_ref[k : k + 1, at]
            sig = jax.nn.sigmoid(out)
            from_scan = dscan[pl.ds(pl.multiple_of(i * 16, 16), 16), :].astype(F32)
            value = (d_conv[h, b, rows, :] + from_scan) * sig * (1.0 + out * (1.0 - sig))
            d_conv[h, b, rows, :] = value
            found = [value] + [value * piece for piece in taken]
            return tuple(c + f[:SUB] + f[SUB:] for c, f in zip(carry, found))

        zero = jnp.zeros((SUB, cols), F32)
        totals = lax.fori_loop(0, all_rows // 16, one, (zero,) * (taps + 1))
        pack[tail_at + taps : tail_at + taps + 1, at] = sums_of(totals[0])
        for k in range(taps):
            pack[tail_at + k : tail_at + k + 1, at] = sums_of(totals[k + 1])

        rim_f[...] = jnp.zeros_like(rim_f)
        for b in range(n_wt):
            for k in range(taps - 1):
                rim_f[b * (taps - 1) + k, :] = d_conv[h, b, k * SUB, :]
        rim_s[h, 0] = rim_f[...].astype(BF16)

        @pl.when(seq == n_seq - 1)
        def _():
            rim_s[h, 1] = jnp.zeros((16, cols), BF16)

        k, copies.count = copies.count, copies.count + 1
        move = pltpu.make_async_remote_copy(
            src_ref=rim_s.at[h, 0], dst_ref=rim_s.at[h, 1], send_sem=send_sems.at[k],
            recv_sem=recv_sems.at[k], device_id=behind, device_id_type=MESH,
        )
        rim_moves.append(move)

        @pl.when(seq > 0)
        def _():
            move.start()

        if h == 0:
            coming["conv"] = load(conv_ref.at[:, :, cols : 2 * cols], conv)
            coming["dscan"] = load(dscan_ref.at[:, cols : 2 * cols], dscan)

    def conv_second(h):
        at = slice(h * cols, (h + 1) * cols)

        @pl.when(seq < n_seq - 1)
        def _():
            rim_moves[h].wait_recv()

        landed = rim_s[h, 1].astype(F32)
        for b in range(n_wt):
            for k in range(taps - 1):
                turned = pltpu.roll(d_conv[h, b, k * SUB : (k + 1) * SUB, :], SUB - 1, 0)
                row = landed[b * (taps - 1) + k : b * (taps - 1) + k + 1, :]
                place = slice(n_rows + k * SUB, n_rows + (k + 1) * SUB)
                d_conv[h, b, place, :] = jnp.where(chunk == SUB - 1, row, turned)

        def one(i, carry):
            b, j = i // (n_rows // 16), i % (n_rows // 16)
            total = jnp.zeros((16, cols), F32)
            for k in range(taps):
                start = pl.multiple_of(j * 16 + (taps - 1 - k) * SUB, SUB)
                total = total + d_conv[h, b, pl.ds(start, 16), :] * wconv_ref[k : k + 1, at]
            draw[pl.ds(pl.multiple_of(i * 16, 16), 16), at] = total.astype(BF16)
            return carry

        lax.fori_loop(0, all_rows // 16, one, 0)

    def early_pieces():
        if ready:
            coming["wout"].wait()
            for k in range(n_wide):
                wout_done(0, k * WIDE, WIDE, k)

    def small_sums():
        coming["u"].wait()
        pack[:LANE, :] = lax.dot_general(
            ddt[...], u_all[...], (((0,), (0,)), ((), ())), preferred_element_type=F32
        )
        for_b = lax.dot_general(
            dbc[...], u_all[...], (((0,), (0,)), ((), ())), preferred_element_type=F32
        )
        pack[2 * LANE : 2 * LANE + 2 * n_state, :] = for_b[: 2 * n_state, :]
        coming["gated"] = load(gated_ref, u_all)
        tile = min(512, n_chan)
        for m in range(0, n_chan, tile):
            fill(small, m // small.shape[-2], pack[:, m : m + tile].T)

    per = cols // d_block
    n_norm = n_feat // cols

    def wide_part(k, block_of):
        part = norm_parts[k % 2]
        if k >= 2:
            take_until(len(seq_groups) + k - 2)
            wide_groups[k - 2].release()
        for b in range(n_wt):
            index = tuple((b >> (wt_bits - 1 - q)) & 1 for q in range(wt_bits))
            for lanes, value in block_of(slice(b * n_rows, (b + 1) * n_rows)):
                part[index + (slice(None), lanes)] = value.astype(BF16)

    def norm(k):
        def block_of(at):
            for part in range(per):
                rows_w = win_rows.at[(k * per + part) % ring]
                value = lax.dot_general(
                    draw[at, :], rows_w[:, :n_chan], (((1,), (1,)), ((), ())),
                    preferred_element_type=F32,
                )
                value = value + lax.dot_general(
                    dgate[at, :], rows_w[:, n_chan:], (((1,), (1,)), ((), ())),
                    preferred_element_type=F32,
                )
                yield slice(part * d_block, (part + 1) * d_block), value

        for part in range(per):
            coming["win", k * per + part].wait()
        wide_part(k, block_of)
        for part in range(per):
            if (k + 1) * per + part < per * n_norm:
                win_block((k + 1) * per + part)

    def out_block(k):
        coming["out", k] = load(w_out_ref.at[:, :, k * cols : (k + 1) * cols], grads.at[k % 2])

    def out(k):
        coming["out", k].wait()
        right = grads[k % 2].reshape(all_rows, cols)

        def block_of(at):
            yield slice(0, cols), jnp.dot(u_all[at, :], right, preferred_element_type=F32)

        wide_part(n_norm + k, block_of)
        if k + 2 < n_norm:
            out_block(k + 2)
        if k + 1 == n_norm:
            for at in range(n_norm):
                block = slice(at * cols, (at + 1) * cols)
                coming["x", at] = load(x_ref.at[:, block], dscan.at[at * n_rows : (at + 1) * n_rows])
                coming["g", at] = load(g_ref.at[:, block], grads.at[0, at])

    def last_of_wide():
        for at in range(n_norm):
            coming["x", at].wait()
            coming["g", at].wait()
        gain = jnp.concatenate([gain_ref[k].astype(F32)[0:1] for k in range(n_wt)], axis=1)
        to = lax.broadcasted_iota(jnp.int32, (n_rows, n_rows), 0)
        source = lax.broadcasted_iota(jnp.int32, (n_rows, n_rows), 1)
        order = (source == (to % steps) * SUB + to // steps).astype(F32)
        for target in (norm_out, out_out):
            for at in range(n_norm):
                block = slice(at * cols, (at + 1) * cols)
                target[:, block] = jnp.dot(
                    order, target[:, block], precision=lax.Precision.HIGHEST,
                    preferred_element_type=F32,
                )

        def one(i, carry):
            rows = pl.ds(pl.multiple_of(i * 16, 16), 16)
            x = jnp.concatenate(
                [
                    dscan[pl.ds(pl.multiple_of(at * n_rows + i * 16, 16), 16), :].astype(F32)
                    for at in range(n_norm)
                ],
                axis=1,
            )
            g = jnp.concatenate([grads[0, at, rows, :].astype(F32) for at in range(n_norm)], axis=1)
            out_out[rows, :] = out_out[rows, :] + x
            inv = lax.rsqrt(jnp.mean(x * x, axis=1, keepdims=True) + EPS)
            scaled = norm_out[rows, :] * gain
            along = jnp.mean(scaled * x, axis=1, keepdims=True)
            norm_out[rows, :] = g + inv * scaled - x * (inv * inv * inv) * along
            return carry

        lax.fori_loop(0, n_rows // 16, one, 0)

    def out_begin():
        coming["gated"].wait()
        out_block(0)
        out_block(1)

    seq_groups = wout_groups + feat_groups + [small_group]
    first_feat = n_wide
    works = [(1.3, functools.partial(wout, 0), [0])]
    works += [(1.5, functools.partial(mixed.middle, bit), []) for bit in range(1, wt_bits)]
    works += [(1.3, functools.partial(wout, k), [k]) for k in range(1, n_wide)]
    works += [
        (4.0, low_pack, []),
        (2.0, early_feat, []),
        (4.5, functools.partial(conv_first, 0), []),
        (4.5, functools.partial(conv_first, 1), []),
        (0.3, early_pieces, []),
        (2.5, lambda: feat(gate_b, dgate[:, cols:]), [first_feat + gate_b]),
        (2.5, functools.partial(conv_second, 0), []),
        (2.5, lambda: feat(conv_a, draw[:, :cols]), [first_feat + conv_a]),
        (2.5, functools.partial(conv_second, 1), []),
        (1.4, lambda: feat(conv_b, draw[:, cols : cols + 256]), [first_feat + conv_b]),
        (1.4, lambda: feat(conv_c, draw[:, cols + 256 :]), [first_feat + conv_c]),
        (4.0, small_sums, [len(seq_groups) - 1]),
    ]
    works += [(2.7, functools.partial(norm, k), [len(seq_groups) + k]) for k in range(n_norm)]
    if not ready:
        gate_first = (3.0, lambda: feat(gate_a, dgate[:, :cols]), [first_feat + gate_a])
        works.insert(len(works) - 14 - n_norm, gate_first)
    works += [(0.2, out_begin, [])]
    works += [(1.5, functools.partial(out, k), [len(seq_groups) + n_norm + k]) for k in range(n_norm)]
    clock, starts_at, ready_at = 5.0, [], {}
    for took, _, readied in works:
        starts_at.append(clock)
        clock += took
        for which in readied:
            ready_at[which] = clock
    all_groups = seq_groups + wide_groups
    entries = []
    for which, group in enumerate(all_groups):
        job = group.members[0]
        axis = "seq" if which < len(seq_groups) else "wt"
        rows = math.prod(job.source.shape[:-1])
        members = [(one.columns.stop - one.columns.start, one.order) for one in group.members]
        entries.append((ready_at[which], axis, rows * 2 / 2**20, members))
    moves = [(29.0, "seq", 1, 0.375), (60.0, "seq", 1, 0.375), (90.0, "seq", 1, 0.14)]
    actions = timetable(entries, moves)
    ended = max(time for time, which, _, _ in actions if which >= len(seq_groups))
    actions.append((ended, None, 0, 0))
    actions.sort(key=lambda action: action[0])

    def take_action(at=0):
        _, which, member, stage = actions.pop(at)
        if which is None:
            last_of_wide()
        else:
            all_groups[which].act(member, stage)

    def take_until(which):
        at = 0
        while at < len(actions):
            if actions[at][1] == which and actions[at][3] <= 1:
                take_action(at)
            else:
                at += 1

    for at, (_, work, _) in zip(starts_at, works):
        while actions and actions[0][0] <= at + 0.01:
            take_action()
        work()
    while actions:
        take_action()
    to_wt(lambda w: gain_sum.at[own_rows(w)], gain_out.at[wt])
    for wait in delivered:
        wait()
    for wait in moved:
        wait()
    for k in range(parts):
        for slot in range(n_wide):
            wout_arrive(k, slot * WIDE, WIDE, slot)
    for move in rim_moves:

        @pl.when(seq > 0)
        def _():
            move.wait_send()

    copies.finish()


def finish_all(
    gated_t, d_gate, d_scan_in, d_raw, inputs, conv, grads, normed_t, w_in, wout, feat, gated,
    w_out, x, g, gain, d_bc, dt_low, w_x, w_dt, w_conv, b_conv, d_rate, a_neg, sums,
):
    n_seq, n_wt = lax.axis_size("seq"), lax.axis_size("wt")
    seq_bits, wt_bits = n_seq.bit_length() - 1, n_wt.bit_length() - 1
    n_chan, all_rows = gated_t.shape
    n_feat, n_rows = normed_t.shape[0], all_rows // n_wt
    n_state, taps = a_neg.shape[0], w_conv.shape[0]
    cols = 512
    parts = parts_of(n_chan, n_seq)
    part_chan = n_chan // parts
    chan_rows, feat_rows, wout_rows = n_chan // n_seq, n_feat // n_seq, part_chan // n_seq
    size = (all_rows + n_rows) // 2
    small_cols, n_wide = 3 * LANE, n_feat // WIDE
    square = ((all_rows, n_chan), BF16)
    blocks = (2,) * seq_bits
    done_type = feat_type(n_feat, n_seq, n_wt)
    plan = feat_plan(n_chan, parts)
    scratch = [
        ((part_chan, all_rows), BF16), square, ((all_rows, cols), BF16), square,
        (normed_t.shape, BF16), ((2, n_wt, n_rows, cols), BF16), ((2, 256, 2 * n_chan), BF16),
        ((n_wt, conv.shape[1], cols), F32), ((2, n_wt, conv.shape[1], cols), F32),
        ((2 * size, LANE), F32), ((size, LANE), F32), ((wt_bits - 1, size, LANE), BF16),
        ((wt_bits - 1, size, LANE), BF16), ((2 * size, LANE), F32), square if parts > 1 else ((16, LANE), BF16), ((all_rows, LANE), BF16), ((all_rows, LANE), BF16),
        ((small_cols, n_chan), F32), ((16, cols), F32), ((2, 2, 16, cols), BF16),
        ((feat_rows, 2 * n_chan), done_type), ((parts, wout_rows, n_feat), BF16),
        ((chan_rows, small_cols), BF16), ((feat_rows, 2 * n_chan), BF16), ((feat_rows, LANE), F32),
        (blocks + (chan_rows, small_cols), BF16),
    ]
    scratch = [pltpu.VMEM(*item) for item in scratch]
    scratch += [pltpu.SemaphoreType.DMA((2, parts, n_wide))]
    scratch += [pltpu.SemaphoreType.DMA((180,))] * 2
    scratch += [pltpu.VMEM(blocks + (wout_rows, WIDE), BF16)] * (n_wide if parts > 1 else 1)
    scratch += [
        pltpu.VMEM(blocks + (feat_rows, width), BF16) for _, width, _ in plan[: 5 - parts % 2 * 2]
    ]
    scratch += [pltpu.VMEM((2,) * wt_bits + (n_rows, cols), BF16)] * 2
    for low in wout_lows(n_wide, True):
        scratch += seq_landings(seq_bits, wout_rows, [WIDE], low)
    for _, width, low in plan:
        scratch += seq_landings(seq_bits, feat_rows, [width], low)
    scratch += seq_landings(seq_bits, chan_rows, [small_cols])
    scratch += landings(wt_bits, n_rows, (cols,) * (2 * n_feat // cols))
    hbm = pl.BlockSpec(memory_space=pl.ANY)
    vmem = pl.BlockSpec(memory_space=pltpu.VMEM)
    return pl.pallas_call(
        functools.partial(finish_kernel, n_seq, n_wt, n_state),
        in_specs=[hbm] * 15 + [vmem] * 10,
        out_specs=[hbm, hbm, hbm, vmem, vmem, hbm],
        out_shape=[
            jax.ShapeDtypeStruct((feat_rows // n_wt, 2 * n_chan * n_wt), done_type),
            jax.ShapeDtypeStruct((parts, wout_rows, n_feat), BF16),
            jax.ShapeDtypeStruct((chan_rows, small_cols), BF16),
            jax.ShapeDtypeStruct((n_rows, n_feat), F32),
            jax.ShapeDtypeStruct((n_rows, n_feat), F32),
            jax.ShapeDtypeStruct((n_wt, feat_rows // n_wt, LANE), F32),
        ],
        scratch_shapes=scratch,
        compiler_params=pltpu.CompilerParams(
            collective_id=1, has_side_effects=True, vmem_limit_bytes=255 * 2**18
        ),
        name="finish_all",
    )(
        gated_t, d_gate, d_scan_in, d_raw, inputs, conv, grads, normed_t, w_in, wout, feat, gated,
        w_out.reshape(grads.shape), x, g, gain, d_bc, dt_low, w_x, w_dt, w_conv, b_conv, d_rate, a_neg, sums,
    )


class Gather:
    def __init__(self, copies, slots, seq, wt, bits):
        self.copies, self.slots, self.seq, self.wt, self.bits = copies, slots, seq, wt, bits
        self.arriving = {}

    def send(self, mask, src):
        slot = self.slots.at[turn(self.wt, mask, self.bits)]
        low = self.bits if mask == 0 else (mask & -mask).bit_length() - 1
        for bit in reversed(range(low)):
            peer = (self.seq, flip(self.wt, bit))
            self.arriving[mask | 1 << bit] = self.copies.remote(src, slot, peer)

    def arrive(self, mask):
        self.arriving[mask].wait_recv()
        self.send(mask, self.slots.at[turn(self.wt, mask, self.bits)])


def start_kernel(
    n_seq, n_wt,
    hidden_ref, grad_ref, gain_ref, starts_ref, win_ref, wout_ref, wconv_ref, bconv_ref, wx_ref,
    wdt_ref, spread_ref, bias_ref, rate_ref,
    normed_out, win_out, conv_out, gate_out, u_out, raw_out, low_out, bcs_out, dgated_out,
    dscan_out, grad_out, gain_out, end_out, lead_out, total_ref, head_ref, tail_ref,
    rows_s, grads_s, gain_s, starts_s, normed_s, win_s, wout_s, conv_s, gate_s, u_s, raw_s, low_s,
    bcs_s, dgated_s, dscan_s, mix_s, fin_s, first_s, half_s, land_s, rim_s, rim_in, normed_t,
    bcb, dec_in, drive_in, g_in, end_s, lead_s, run_s, span_s, own_span, gap_s, edge_send, edge_land, span_send,
    span_land,
    send_sems, recv_sems, join_send, join_recv,
):
    seq, wt = lax.axis_index("seq"), lax.axis_index("wt")
    bits = n_wt.bit_length() - 1
    n_rows, n_feat = hidden_ref.shape
    n_chan, shard = wout_ref.shape[0], win_ref.shape[0]
    taps = wconv_ref.shape[0]
    rim = (taps - 1) * SUB
    all_rows = n_wt * n_rows
    near_y, near_z = (flip(seq, 0), wt), (flip(seq, 1), wt)
    wt_peers = [(seq, turn(wt, mask, bits)) for mask in range(1, n_wt)]
    ahead, behind = (lax.rem(seq + 1, n_seq), wt), (lax.rem(seq + n_seq - 1, n_seq), wt)

    barrier = pltpu.get_barrier_semaphore()
    partners = wt_peers + [near_y, near_z, ahead, behind]
    for r in range(1, n_seq.bit_length() - 1):
        partners += [(lax.rem(seq + d, n_seq), wt) for d in (2**r, n_seq - 2**r)]
    for partner in partners:
        pl.semaphore_signal(barrier, inc=1, device_id=partner, device_id_type=MESH)
    pl.semaphore_wait(barrier, len(partners))

    copies = Copies(send_sems, recv_sems)
    part = shard // 4
    quarter = seq % 4

    def win_part(owner, which, at, rows, half):
        start = pl.multiple_of(owner * shard + which * part + at, 16)
        return win_s.at[pl.ds(start, rows), half * n_chan : (half + 1) * n_chan]

    def send_far(half):
        found = {}
        rows = pl.ds(pl.multiple_of(quarter * part, 16), part)
        for mask in range(2, n_wt):
            to = turn(wt, mask, bits)
            columns = pl.ds(pl.multiple_of((half * n_wt + to) * n_chan, LANE), n_chan)
            found[mask] = copies.remote(
                win_ref.at[rows, columns], win_part(wt, quarter, 0, part, half), (seq, to)
            )
        return found

    def send_near(half):
        to = flip(wt, 0)
        place = win_s.at[
            pl.ds(pl.multiple_of(wt * shard, 16), shard), half * n_chan : (half + 1) * n_chan
        ]
        columns = pl.ds(pl.multiple_of((half * n_wt + to) * n_chan, LANE), n_chan)
        own = pl.ds(pl.multiple_of((half * n_wt + wt) * n_chan, LANE), n_chan)
        return (
            copies.remote(win_ref.at[:, columns], place, (seq, to)),
            copies.local(win_ref.at[:, own], place),
        )

    def share_first(half, found):
        passed = {}
        for mask, copy in found.items():
            copy.wait_recv()
            block = win_part(turn(wt, mask, bits), quarter, 0, part, half)
            passed[mask] = (
                copies.remote(block, block, near_y), copies.remote(block, block, near_z)
            )
        return passed

    def share_second(half, passed):
        last = []
        for mask, (by_y, by_z) in passed.items():
            owner = turn(wt, mask, bits)
            by_z.wait_recv()
            block = win_part(owner, flip(quarter, 1), 0, part // 2, half)
            last.append(copies.remote(block, block, near_y))
            by_y.wait_recv()
            block = win_part(owner, flip(quarter, 0), part // 2, part // 2, half)
            last.append(copies.remote(block, block, near_z))
        return last

    def normalise(mask):
        at = turn(wt, mask, bits)
        gain = jnp.concatenate(
            [gain_s[k].astype(F32)[0:1] for k in range(n_wt)], axis=1
        )

        def body(i, carry):
            rows = pl.ds(pl.multiple_of(i * 16, 16), 16)
            x = rows_s[at, rows, :].astype(F32)
            inv = lax.rsqrt(jnp.mean(x * x, axis=1, keepdims=True) + EPS)
            place = pl.ds(pl.multiple_of(at * n_rows + i * 16, 16), 16)
            normed_s[place, :] = (x * inv * gain).astype(BF16)
            return carry

        lax.fori_loop(0, n_rows // 16, body, 0)

    far = send_far(0)
    rows = Gather(copies, rows_s, seq, wt, bits)
    gains = Gather(copies, gain_s, seq, wt, bits)
    starts = Gather(copies, starts_s, seq, wt, bits)
    own_copies = [
        copies.local(gain_ref, gain_s.at[wt]),
        copies.local(starts_ref, starts_s.at[wt]),
        copies.local(hidden_ref, rows_s.at[wt]),
    ]
    gains.send(0, gain_ref)
    rows.send(0, hidden_ref)
    near = send_near(0)
    starts.send(0, starts_ref)
    wout_copy = copies.local(wout_ref, wout_s)
    for mask in range(n_wt - 1, 0, -1):
        if mask in gains.arriving:
            gains.arrive(mask)
    for mask in range(1, n_wt):
        if mask not in (1, 2):
            gains.arriving[mask].wait_recv()
    for copy in own_copies:
        copy.wait()
    normalise(0)
    rows.arrive(1)
    normalise(1)
    passed = share_first(0, far)
    far = send_far(1)
    last = share_second(0, passed)
    near_gate = send_near(1)
    for mask in range(2, n_wt):
        rows.arrive(mask)
        if mask == 2:
            half_rows = n_rows // 2
            tops = Gather(copies, grads_s.at[:, :half_rows], seq, wt, bits)
            ends = Gather(copies, grads_s.at[:, half_rows:], seq, wt, bits)
            grad_copy = copies.local(grad_ref, grads_s.at[wt])
            tops.send(0, grad_ref.at[:half_rows])
        normalise(mask)
    results = [copies.local(gain_s, gain_out)]
    near[0].wait_recv()
    near[1].wait()
    for copy in last:
        copy.wait_recv()

    n_block, m_block = 256, 512

    def tiles(body):
        m_count = all_rows // m_block

        def one(i, carry):
            m = pl.multiple_of((i % m_count) * m_block, m_block)
            n = pl.multiple_of((i // m_count) * n_block, n_block)
            body(m, n)
            return carry

        lax.fori_loop(0, m_count * (n_chan // n_block), one, 0)

    def conv_tile(m, n):
        value = jnp.dot(
            normed_s[pl.ds(m, m_block), :], win_s[:, pl.ds(n, n_block)], preferred_element_type=F32
        )
        value = value.astype(BF16).astype(F32)
        for k in range(m_block // n_rows):
            conv_s[m // n_rows + k, rim:, pl.ds(n, n_block)] = value[k * n_rows : (k + 1) * n_rows]

    tiles(conv_tile)

    rim_s[...] = jnp.zeros_like(rim_s)
    for b in range(n_wt):
        for k in range(taps - 1):
            at = rim + n_rows - (taps - 1 - k) * SUB
            rim_s[b * (taps - 1) + k, :] = conv_s[b, at + SUB - 1, :]
    rim_s2 = rim_s[...].astype(BF16)
    rim_in[0] = rim_s2

    @pl.when(seq == 0)
    def _():
        rim_in[1] = jnp.zeros_like(rim_s2)

    k_rim, copies.count = copies.count, copies.count + 1
    rim_copy = pltpu.make_async_remote_copy(
        src_ref=rim_in.at[0], dst_ref=rim_in.at[1], send_sem=send_sems.at[k_rim],
        recv_sem=recv_sems.at[k_rim], device_id=ahead, device_id_type=MESH,
    )

    @pl.when(seq < n_seq - 1)
    def _():
        rim_copy.start()

    passed = share_first(1, far)

    def convolve(b, j):
        rows = pl.ds(pl.multiple_of(j * 16, 16), 16)
        total = bconv_ref[...] + conv_s[b, rows, :] * wconv_ref[0:1, :]
        for k in range(1, taps):
            at = pl.ds(pl.multiple_of(j * 16 + k * SUB, SUB), 16)
            total = total + conv_s[b, at, :] * wconv_ref[k : k + 1, :]
        place = pl.ds(pl.multiple_of(b * n_rows + j * 16, 16), 16)
        u_s[place, :] = (total * jax.nn.sigmoid(total)).astype(BF16)

    head = -(-(taps - 1) // 2)
    pairs = n_rows // 16

    def convolve_tail(i, carry):
        convolve(i // (pairs - head), head + i % (pairs - head))
        return carry

    lax.fori_loop(0, n_wt * (pairs - head), convolve_tail, 0)

    @pl.when(seq > 0)
    def _():
        rim_copy.wait_recv()

    rim_rows = rim_in[1].astype(F32)
    first = lax.broadcasted_iota(jnp.int32, (SUB, n_chan), 0) == 0
    for b in range(n_wt):
        for k in range(taps - 1):
            at = rim + n_rows - (taps - 1 - k) * SUB
            moved = pltpu.roll(conv_s[b, at : at + SUB, :], 1, 0)
            row = rim_rows[b * (taps - 1) + k : b * (taps - 1) + k + 1, :]
            conv_s[b, k * SUB : (k + 1) * SUB, :] = jnp.where(first, row, moved)
    lax.fori_loop(0, n_wt * head, lambda i, c: (convolve(i // head, i % head), c)[1], 0)
    results += [copies.local(conv_s, conv_out), copies.local(u_s, u_out)]

    packed = []
    for b in range(n_wt):
        block = u_s[b * n_rows : (b + 1) * n_rows, :]
        mix_s[b * n_rows : (b + 1) * n_rows, :] = jnp.dot(
            block, wx_ref[:, :LANE], preferred_element_type=F32
        )
        packed.append(jnp.dot(block, wx_ref[:, LANE:], preferred_element_type=F32))
    mix_s[all_rows:, :] = jnp.concatenate(packed, axis=1)
    mixed = WtSum(copies, mix_s, first_s, half_s, land_s, fin_s, seq, wt, bits)
    mixed.begin()
    last = share_second(1, passed)
    starts.arrive(2)

    def transpose(b):
        at = slice(b * n_rows, (b + 1) * n_rows)
        normed_t[:, at] = normed_s[at, :].T

    transpose(0)
    for bit in range(1, bits):
        mixed.middle(bit)
    ends.send(0, grad_ref.at[half_rows:])
    for b in range(1, n_wt):
        transpose(b)
    results.append(copies.local(normed_t, normed_out))
    mixed.end()

    low_s[...] = fin_s[:all_rows, :].astype(BF16)
    starts.arriving[1].wait_recv()
    starts.arriving[3].wait_recv()
    lane = lax.broadcasted_iota(jnp.int32, (n_rows, LANE), 1)
    width = LANE // n_wt
    for b in range(n_wt):
        moved = fin_s[all_rows:, :]
        if b:
            moved = pltpu.roll(moved, LANE - b * width, 1)
        bcs_s[b * n_rows : (b + 1) * n_rows, :] = (
            jnp.where(lane < width, moved, 0.0).astype(BF16) + starts_s[b]
        )

    def raw_tile(m, n):
        value = lax.dot_general(
            low_s[pl.ds(m, m_block), :], wdt_ref[pl.ds(n, n_block), :], (((1,), (1,)), ((), ())),
            preferred_element_type=F32,
        )
        raw_s[pl.ds(m, m_block), pl.ds(n, n_block)] = value.astype(BF16)

    tiles(raw_tile)
    results += [
        copies.local(low_s, low_out), copies.local(bcs_s, bcs_out), copies.local(raw_s, raw_out)
    ]

    near_gate[0].wait_recv()
    near_gate[1].wait()
    for copy in last:
        copy.wait_recv()
    results.append(copies.local(win_s, win_out))

    def gate_tile(m, n):
        value = jnp.dot(
            normed_s[pl.ds(m, m_block), :], win_s[:, pl.ds(n_chan + n, n_block)],
            preferred_element_type=F32,
        )
        gate_s[pl.ds(m, m_block), pl.ds(n, n_block)] = value.astype(BF16)

    tiles(gate_tile)
    results.append(copies.local(gate_s, gate_out))
    n_state = rate_ref.shape[0]
    width = dec_in.shape[1]
    steps = n_rows // SUB
    start_at = 2 * n_state * LANE

    def stream_of(i):
        base = wt + (i // 2) * (1 - 2 * bit_of(wt, 1)) * 2
        return base + (i % 2) * (1 - 2 * bit_of(wt, 0))

    def back(b):
        at = pl.ds(pl.multiple_of(b * n_rows, n_rows), n_rows)

        def one(i, carry):
            n = pl.ds(pl.multiple_of(i * n_block, n_block), n_block)
            d_gated = lax.dot_general(
                grads_s[b], wout_s[n, :], (((1,), (1,)), ((), ())), preferred_element_type=F32
            )
            gate = gate_s[at, n].astype(F32)
            dgated_s[at, n] = d_gated
            dscan_s[at, n] = (d_gated * gate * jax.nn.sigmoid(gate)).astype(BF16)
            return carry

        lax.fori_loop(0, n_chan // n_block, one, 0)

    def chunk_ends(b, part):
        columns = pl.ds(pl.multiple_of(part * width, width), width)

        def prepare(j, total):
            rows = pl.ds(pl.multiple_of(j * 16, 16), 16)
            at = pl.ds(pl.multiple_of(b * n_rows + j * 16, 16), 16)
            delta = softplus(raw_s[at, columns].astype(F32) + bias_ref[:, columns])
            held = jnp.where(wide(bcb[rows, start_at : start_at + LANE], width) > 0.5, RESET, delta)
            dec_in[rows, :] = held
            drive_in[rows, :] = delta * u_s[at, columns].astype(F32)
            g_in[rows, :] = dscan_s[at, columns].astype(F32)
            return total + held[:SUB] + held[SUB:]

        total = lax.fori_loop(0, steps // 2, prepare, jnp.zeros((SUB, width), F32))
        total_ref[b, :, columns] = total
        span = jnp.sum(total, 0, keepdims=True)
        span_s[b, :, columns] = span
        for first_n in range(0, n_state, 2):
            states = range(first_n, first_n + 2)

            def step(j, carry):
                rows = pl.ds(pl.multiple_of(j * SUB, SUB), SUB)
                held, drive, g = dec_in[rows, :], drive_in[rows, :], g_in[rows, :]
                running, products, passed = [], [], []
                for n, h, so_far, p in zip(states, *carry):
                    b_row = wide(bcb[rows, n * LANE : (n + 1) * LANE], width)
                    c_row = wide(bcb[rows, (n_state + n) * LANE : (n_state + n + 1) * LANE], width)
                    decay = jnp.exp2(held * rate_ref[n : n + 1, columns])
                    so_far = so_far * decay
                    running.append(decay * h + drive * b_row)
                    products.append(so_far)
                    passed.append(p + so_far * (g * c_row))
                return tuple(running), tuple(products), tuple(passed)

            zero = tuple(jnp.zeros((SUB, width), F32) for _ in states)
            one = tuple(jnp.ones((SUB, width), F32) for _ in states)
            carry = lax.fori_loop(0, steps, step, (zero, one, zero), unroll=8)
            for n, h, decay, p in zip(states, *carry):
                end = chunk_prefix(decay, h, False)[1]
                lead = chunk_prefix(decay, p, True)[1]
                end_s[b, n, :, columns], lead_s[b, n, :, columns] = end, lead
                run_s[0, b, n : n + 1, columns] = end[SUB - 1 :]
                run_s[1, b, n : n + 1, columns] = lead[:1]

    def ends_of(i, carry):
        b = stream_of(i)
        back(b)
        bcb[...] = jnp.dot(
            bcs_s[pl.ds(pl.multiple_of(b * n_rows, n_rows), n_rows), :], spread_ref[...],
            preferred_element_type=F32,
        )
        lax.fori_loop(0, n_chan // width, lambda part, c: (chunk_ends(b, part), c)[1], 0)
        return carry

    grad_copy.wait()
    tops.arrive(1)
    ends.arrive(1)
    wout_copy.wait()
    lax.fori_loop(0, 2, ends_of, 0)
    for mask in range(2, n_wt):
        tops.arrive(mask)
        ends.arrive(mask)
        ends_of(mask, 0)
    results.append(copies.local(grads_s, grad_out))
    results += [copies.local(dgated_s, dgated_out), copies.local(dscan_s, dscan_out)]
    results += [copies.local(end_s, end_out), copies.local(lead_s, lead_out)]
    join_rounds(
        n_seq, n_wt, seq, wt, rate_ref[...], head_ref, tail_ref, run_s, span_s, own_span, gap_s,
        edge_send, edge_land, span_send, span_land, join_send, join_recv,
    )
    for copy in results:
        copy.wait()

    @pl.when(seq < n_seq - 1)
    def _():
        rim_copy.wait_send()

    copies.finish()


def start_all(
    hidden, grad, gain, starts, w_in, w_out, w_conv, b_conv, w_x, w_dt, bias, rate_rows
):
    n_seq, n_wt = lax.axis_size("seq"), lax.axis_size("wt")
    n_rows, n_feat = hidden.shape
    n_chan, taps = w_out.shape[0], w_conv.shape[0]
    rows, rim = n_wt * n_rows, (taps - 1) * SUB
    shapes = [
        ((n_feat, rows), BF16), ((n_feat, 2 * n_chan), BF16), ((n_wt, rim + n_rows, n_chan), F32),
        ((rows, n_chan), BF16), ((rows, n_chan), BF16), ((rows, n_chan), BF16), ((rows, LANE), BF16),
        ((rows, LANE), BF16), ((rows, n_chan), F32), ((rows, n_chan), BF16),
        ((n_wt, n_rows, n_feat), BF16), ((n_wt,) + gain.shape, BF16),
        ((n_wt, rate_rows.shape[0], SUB, n_chan), F32),
        ((n_wt, rate_rows.shape[0], SUB, n_chan), F32), ((n_wt, SUB, n_chan), F32),
        ((n_wt,) + rate_rows.shape, F32), ((n_wt,) + rate_rows.shape, F32),
    ]
    normed, win, conv, gate, u, raw, low, bcs, dgated, dscan, grads, gains = shapes[:12]
    ends = shapes[12]
    n_state, rounds = rate_rows.shape[0], n_seq.bit_length() - 1
    count = (2 * n_state + 1) * LANE
    width = min(512, n_chan)
    spans, edges = (2 * n_wt, n_chan), (n_wt, n_state, n_chan)
    size = (rows + n_rows) // 2
    bits = n_wt.bit_length() - 1
    scratch = [
        grads, grads, gains, ((n_wt, n_rows, LANE), BF16), ((rows, n_feat), BF16), win, (w_out.shape, BF16), conv,
        gate, u, raw, low, bcs, dgated, dscan, ((2 * size, LANE), F32), ((2 * size, LANE), F32),
        ((size, LANE), F32), ((bits, size, LANE), BF16), ((bits, size, LANE), BF16),
        ((16, n_chan), F32),
        ((2, 16, n_chan), BF16), normed,
        ((n_rows, count), F32), ((n_rows, width), F32), ((n_rows, width), F32), ((n_rows, width), F32),
        ends, ends, ((2,) + edges, F32), ((n_wt, 1, n_chan), F32), (spans, F32), (spans, F32),
        ((2, 2) + edges, BF16),
        ((rounds, 2) + edges, BF16), ((rounds,) + spans, F32), ((rounds, 2) + spans, F32),
    ]
    hbm = pl.BlockSpec(memory_space=pl.ANY)
    vmem = pl.BlockSpec(memory_space=pltpu.VMEM)
    return pl.pallas_call(
        functools.partial(start_kernel, n_seq, n_wt),
        in_specs=[hbm] * 6 + [vmem] * 7,
        out_specs=[hbm] * (len(shapes) - 3) + [vmem] * 3,
        out_shape=[jax.ShapeDtypeStruct(*item) for item in shapes],
        scratch_shapes=[pltpu.VMEM(*item) for item in scratch]
        + [pltpu.SemaphoreType.DMA((90,))] * 2
        + [pltpu.SemaphoreType.DMA((rounds, 2, 2))] * 2,
        compiler_params=pltpu.CompilerParams(
            collective_id=2, has_side_effects=True, vmem_limit_bytes=4090 * 2**14
        ),
        name="start_all",
    )(
        hidden, grad, gain, starts, w_in, w_out, w_conv, b_conv, w_x, w_dt, spread_matrix(n_state),
        bias, rate_rows,
    )


def dot(left, right, left_dim=1, right_dim=0):
    return lax.dot_general(
        left, right, (((left_dim,), (right_dim,)), ((), ())), preferred_element_type=F32
    )


def to_chunks(rows):
    n_rows, width = rows.shape
    return rows.reshape(SUB, n_rows // SUB, width).swapaxes(0, 1).reshape(n_rows, width)


def per_device(
    hidden_in, doc_starts, norm_gain, in_weight, conv_weight, conv_bias, x_weight,
    dt_weight, dt_bias, a_log, d_skip, out_weight, grad_output,
):
    n_wt, n_seq = lax.axis_size("wt"), lax.axis_size("seq")
    seq_at = lax.axis_index("seq")
    n_chan = out_weight.shape[0]
    taps = conv_weight.shape[1]
    dt_rank = dt_weight.shape[1]
    n_state = a_log.shape[1]
    rows_own = hidden_in[0]
    n_rows, n_feat = rows_own.shape
    steps = n_rows // SUB

    w_conv = conv_weight.astype(F32)
    starts = jnp.pad(
        to_chunks(doc_starts[0].astype(BF16)[:, None]), ((0, 0), (2 * n_state, LANE - 2 * n_state - 1))
    )
    rates = (-LOG2E * jnp.exp(a_log.astype(F32))).T
    bias = dt_bias.astype(F32)[None]
    skip = d_skip.astype(F32)[None]
    (
        normed_t, w_in, padded, gate_in, inputs, dt_raw, dt_low, bcs, d_gated, d_scanned, grad_all, gains,
        ends, leads, totals, head, tail,
    ) = start_all(
        to_chunks(rows_own), to_chunks(grad_output[0]),
        jnp.broadcast_to(norm_gain[None], (16, norm_gain.shape[0])), starts, in_weight, out_weight,
        w_conv.T, conv_bias.astype(F32)[None], x_weight, dt_weight, bias,
        rates,
    )
    gain = gains[:, 0].reshape(n_feat).astype(F32)

    gated, gated_t, d_gate, d_scan_in, d_raw, d_bc, d_rate, sums, wout, feat = scan_all(
        bcs, dt_raw, inputs, d_scanned, gate_in, d_gated, bias, skip, rates,
        ends, leads, totals, head, tail, grad_all.reshape(n_wt * n_rows, n_feat), normed_t,
    )


    feat_grads, d_wout, small, input_grad, output, gain_parts = finish_all(
        gated_t, d_gate, d_scan_in, d_raw, inputs, padded, grad_all, normed_t, w_in, wout, feat,
        gated, out_weight, rows_own, grad_output[0], gains, d_bc, dt_low, x_weight, dt_weight, w_conv.T,
        conv_bias.astype(F32)[None], d_rate, rates, sums,
    )
    d_wout = d_wout.reshape(-1, n_feat).astype(F32)
    small = small.astype(F32)
    widths = (dt_rank, dt_rank, 2 * n_state, n_state, taps, 1, 1, 1)
    cuts, at = [], 0
    for piece in widths:
        cuts.append(small[:, at : at + piece])
        at += piece
    d_wx, d_wdt, d_wbc, d_loga, d_wconv, d_bconv, d_bdt, d_skips = cuts
    own = n_feat // (n_seq * n_wt)
    own_at = own * (n_wt * seq_at + lax.axis_index("wt"))
    gain_grad = jnp.sum(gain_parts, (0, 2)) / lax.dynamic_slice_in_dim(gain, own_at, own, 0)
    return (
        output[None],
        input_grad[None],
        gain_grad,
        feat_grads.astype(F32),
        d_wconv,
        d_bconv[:, 0],
        jnp.concatenate([d_wx, d_wbc], 1),
        d_wdt,
        d_bdt[:, 0],
        d_loga,
        d_skips[:, 0],
        d_wout,
    )


def solution(mesh):
    placed = (
        P("wt", "seq", None),
        P("wt", "seq"),
        P("wt"),
        P("wt", None),
        P("wt", None),
        P("wt"),
        P("wt", None),
        P("wt", None),
        P("wt"),
        P("wt", None),
        P("wt"),
        P("wt", None),
        P("wt", "seq", None),
    )
    every = ("seq", "wt")
    return jax.shard_map(
        per_device,
        mesh=mesh,
        in_specs=placed,
        out_specs=(
            P("wt", "seq", None),
            P("wt", "seq", None),
            P(every),
            P(every, None),
            P(every, None),
            P(every),
            P(every, None),
            P(every, None),
            P(every),
            P(every, None),
            P(every),
            P(every, None),
        ),
        check_vma=False,
    )
```

profile of v0, /device:TPU:0, one launch (start us, length us, event | category | flops | bytes accessed | tf_op | source)
XLA Modules:
  0.0 419.4 jit_solution(3514426436851773350)
XLA Ops:
  0.6 1.4 multiply_bitcast_fusion.rate_ref.a_ref
  2.1 4.1 copy_bitcast_fusion
  6.1 1.0 copy.40.wx_ref
  7.1 0.6 convert_bitcast_fusion.wconv_ref
  7.7 0.6 broadcast_in_dim.37
  9.2 0.7 pad.4.starts_ref
  10.0 0.6 broadcast_in_dim.28.gain_ref
  10.6 148.9 %start_all.1 = (bf16[2048,1024]{1,0:T(8,128)(2,1)}, bf16[2048,2048]{1,0:T(8,128)(2,1)}, f32[4,280,1024]{2,1,0:T(8,128)}, bf16[1024,1024]{1,0:T(8,128)(2,1)}, bf1...) custom-call(bf16[256,2048]{1,0:T(8,128)(2,1)} %get-tuple-element.108, ...), custom_call_target="tpu_custom_call" | custom-call | tf_op jit(solution)/shard_map/start_all/pallas_call | solution.py:1966
  159.5 0.6 broadcast_in_dim.39
  160.1 104.4 %scan_all.1 = (bf16[1024,1024]{1,0:T(8,128)(2,1)}, bf16[1024,1024]{1,0:T(8,128)(2,1)}, bf16[1024,1024]{1,0:T(8,128)(2,1)}, bf16[1024,1024]{1,0:T(8,128)(2,1)}, b...) custom-call(bf16[1024,128]{1,0:T(8,128)(2,1)} %get-tuple-element.45., ...), custom_call_target="tpu_custom_call" | custom-call | tf_op jit(solution)/shard_map/scan_all/pallas_call | solution.py:794
  264.5 139.4 %finish_all.1 = (bf16[64,8192]{1,0:T(8,128)(2,1)}, bf16[2,64,2048]{2,1,0:T(8,128)(2,1)}, bf16[128,384]{1,0:T(8,128)(2,1)}, f32[256,2048]{1,0:T(8,128)}, f32[256,2048]{1,0:T(8,128)}, /*index=5*/f32[4,64,128]{2,1,0:T(8,128)}) custom-call(bf16[1024,1024]{1,0:T(8,128)(2,1)} %get-tuple-element.58.gated_t_ref, bf16[1024,1024]{1,0:T(8,128)(2,1)} %get-tuple-element.59.dgate_ref, ...), custom_call_target="tpu_custom_call" | custom-call | tf_op jit(solution)/shard_map/finish_all/pallas_call | solution.py:1495
  403.9 1.5 fusion
  405.4 0.8 slice.39
  406.2 0.7 copy.43
  406.9 1.0 reduce_sum.9
  407.9 0.8 slice_convert_fusion
  409.3 2.8 convert_element_type.46
  412.1 1.1 bitcast_convert_fusion
  413.3 0.7 slice_reduce_fusion
  414.1 0.7 copy.44
  414.9 0.7 copy.42
  415.5 1.3 copy.49
  416.8 1.0 copy-done
  417.9 1.3 copy.50
  (31 shorter events, 1.7 us)
Async XLA Ops:
  2.0 4.1 copy-start.4
  2.1 5.1 %copy-start.5 = (bf16[1024,4]{0,1:T(4,128)(2,1)S(1)}, bf16[1024,4]{0,1:T(4,128)(2,1)}, u32[]{:S(2)}) copy-start(bf16[1024,4]{0,1:T(4,128)(2,1)} %param.20) | copy-start | bytes 24580
  2.1 5.7 %copy-start.6 = (bf16[1024]{0:T(1024)(128)(2,1)S(1)}, bf16[1024]{0:T(1024)(128)(2,1)}, u32[]{:S(2)}) copy-start(bf16[1024]{0:T(1024)(128)(2,1)} %param.21) | copy-start | bytes 6148
  2.1 6.3 %copy-start.7 = (bf16[1024]{0:T(1024)(128)(2,1)S(1)}, bf16[1024]{0:T(1024)(128)(2,1)}, u32[]{:S(2)}) copy-start(bf16[1024]{0:T(1024)(128)(2,1)} %param.24) | copy-start | bytes 6148
  2.1 6.9 %copy-start.10 = (s32[1,256]{1,0:T(1,128)S(1)}, s32[1,256]{1,0:T(1,128)}, u32[]{:S(2)}) copy-start(s32[1,256]{1,0:T(1,128)} %param.17) | copy-start | bytes 3076
  2.1 7.9 %copy-start.9 = (bf16[512]{0:T(512)(128)(2,1)S(1)}, bf16[512]{0:T(512)(128)(2,1)}, u32[]{:S(2)}) copy-start(bf16[512]{0:T(512)(128)(2,1)} %param.18) | copy-start | bytes 3076
  10.6 148.9 %copy-start.8 = (bf16[1024]{0:T(1024)(128)(2,1)S(1)}, bf16[1024]{0:T(1024)(128)(2,1)}, u32[]{:S(2)}) copy-start(bf16[1024]{0:T(1024)(128)(2,1)} %param.26) | copy-start | bytes 6148
  403.9 8.2 %copy-start.3 = (bf16[2,64,2048]{2,1,0:T(8,128)(2,1)S(1)}, bf16[2,64,2048]{2,1,0:T(8,128)(2,1)}, u32[]{:S(2)}) copy-start(bf16[2,64,2048]{2,1,0:T(8,128)(2,1)} %get-tuple-element.77) | copy-start | bytes 1572868
  409.3 4.0 copy-start.2
  409.3 6.2 %copy-start.1 = (f32[256,2048]{1,0:T(8,128)S(1)}, f32[256,2048]{1,0:T(8,128)}, u32[]{:S(2)}) copy-start(f32[256,2048]{1,0:T(8,128)} %get-tuple-element.72) | copy-start | bytes 6291460
  415.5 2.3 copy-start
where the time goes:
time: 423 us; the launch traced here: 419 us
  Pallas kernels  393 us (93%)
  local copies, waits for them, and re-layouts  15.6 us (4%)
  other arithmetic  10.2 us (2%)
    pallas_call x1, Pallas kernels, start_all(): pl.pallas_call(functools.partial(start_kernel, n_seq, n_wt), in_specs=[hb...  149 us
    pallas_call x1, Pallas kernels, finish_all(): pl.pallas_call(functools.partial(finish_kernel, n_seq, n_wt, n_state), in...  139 us
    pallas_call x1, Pallas kernels, scan_all(): pl.pallas_call(functools.partial(scan_kernel, n_state, n_seq, parts), gri...  104 us

commit v1 on v0

--- a/solution.py
+++ b/solution.py
@@ -584,7 +584,7 @@
         g_in[rows, :] = g_ref[rows, :].astype(F32)
         return carry
 
-    lax.fori_loop(0, steps // 2, prepare, 0)
+    lax.fori_loop(0, steps // 2, prepare, 0, unroll=2)
     chunk = lax.broadcasted_iota(jnp.int32, (SUB, width), 0)
     total = total_ref[0]
     before, after = total, total
@@ -672,7 +672,7 @@
         return bias_sum + d_pre[:SUB] + d_pre[SUB:], skip_sum + gu[:SUB] + gu[SUB:]
 
     zero = jnp.zeros((SUB, width), F32)
-    bias_sum, skip_sum = lax.fori_loop(0, steps // 2, finish, (zero, zero))
+    bias_sum, skip_sum = lax.fori_loop(0, steps // 2, finish, (zero, zero), unroll=2)
     gated_t_ref[...] = gated_ref[...].T
     if parts > 1:
         gated_s, dgate_s = scratch[:2]
@@ -1630,7 +1630,7 @@
             normed_s[place, :] = (x * inv * gain).astype(BF16)
             return carry
 
-        lax.fori_loop(0, n_rows // 16, body, 0)
+        lax.fori_loop(0, n_rows // 16, body, 0, unroll=2)
 
     far = send_far(0)
     rows = Gather(copies, rows_s, seq, wt, bits)
@@ -1739,7 +1739,7 @@
         convolve(i // (pairs - head), head + i % (pairs - head))
         return carry
 
-    lax.fori_loop(0, n_wt * (pairs - head), convolve_tail, 0)
+    lax.fori_loop(0, n_wt * (pairs - head), convolve_tail, 0, unroll=2)
 
     @pl.when(seq > 0)
     def _():
@@ -1859,7 +1859,7 @@
             g_in[rows, :] = dscan_s[at, columns].astype(F32)
             return total + held[:SUB] + held[SUB:]
 
-        total = lax.fori_loop(0, steps // 2, prepare, jnp.zeros((SUB, width), F32))
+        total = lax.fori_loop(0, steps // 2, prepare, jnp.zeros((SUB, width), F32), unroll=2)
         total_ref[b, :, columns] = total
         span = jnp.sum(total, 0, keepdims=True)
         span_s[b, :, columns] = span

time: 423 us -> 419 us (level)
  no operation moved by 1% of the time
where the time goes in v1:
time: 419 us; the launch traced here: 416 us
  Pallas kernels  390 us (93%)
  local copies, waits for them, and re-layouts  15.6 us (4%)
  other arithmetic  10.2 us (2%)
    pallas_call x1, Pallas kernels, start_all(): pl.pallas_call(functools.partial(start_kernel, n_seq, n_wt), in_specs=[hb...  147 us
    pallas_call x1, Pallas kernels, finish_all(): pl.pallas_call(functools.partial(finish_kernel, n_seq, n_wt, n_state), in...  138 us
    pallas_call x1, Pallas kernels, scan_all(): pl.pallas_call(functools.partial(scan_kernel, n_state, n_seq, parts), gri...  105 us

profile of v1, /device:TPU:0, one launch (start us, length us, event | category | flops | bytes accessed | tf_op | source)
XLA Modules:
  0.0 416.5 jit_solution(13685624639522072259)
XLA Ops:
  0.6 1.4 multiply_bitcast_fusion.rate_ref.a_ref
  2.1 4.1 copy_bitcast_fusion
  6.1 1.0 copy.40.wx_ref
  7.1 0.6 convert_bitcast_fusion.wconv_ref
  7.7 0.6 broadcast_in_dim.37
  9.2 0.7 pad.4.starts_ref
  10.0 0.6 broadcast_in_dim.28.gain_ref
  10.6 147.1 %start_all.1 = (bf16[2048,1024]{1,0:T(8,128)(2,1)}, bf16[2048,2048]{1,0:T(8,128)(2,1)}, f32[4,280,1024]{2,1,0:T(8,128)}, bf16[1024,1024]{1,0:T(8,128)(2,1)}, bf1...) custom-call(bf16[256,2048]{1,0:T(8,128)(2,1)} %get-tuple-element.108, ...), custom_call_target="tpu_custom_call" | custom-call | tf_op jit(solution)/shard_map/start_all/pallas_call | solution.py:1966
  157.7 0.6 broadcast_in_dim.39
  158.3 104.6 %scan_all.1 = (bf16[1024,1024]{1,0:T(8,128)(2,1)}, bf16[1024,1024]{1,0:T(8,128)(2,1)}, bf16[1024,1024]{1,0:T(8,128)(2,1)}, bf16[1024,1024]{1,0:T(8,128)(2,1)}, b...) custom-call(bf16[1024,128]{1,0:T(8,128)(2,1)} %get-tuple-element.45., ...), custom_call_target="tpu_custom_call" | custom-call | tf_op jit(solution)/shard_map/scan_all/pallas_call | solution.py:794
  262.9 138.2 %finish_all.1 = (bf16[64,8192]{1,0:T(8,128)(2,1)}, bf16[2,64,2048]{2,1,0:T(8,128)(2,1)}, bf16[128,384]{1,0:T(8,128)(2,1)}, f32[256,2048]{1,0:T(8,128)}, f32[256,2048]{1,0:T(8,128)}, /*index=5*/f32[4,64,128]{2,1,0:T(8,128)}) custom-call(bf16[1024,1024]{1,0:T(8,128)(2,1)} %get-tuple-element.58.gated_t_ref, bf16[1024,1024]{1,0:T(8,128)(2,1)} %get-tuple-element.59.dgate_ref, ...), custom_call_target="tpu_custom_call" | custom-call | tf_op jit(solution)/shard_map/finish_all/pallas_call | solution.py:1495
  401.0 1.5 fusion
  402.5 0.8 slice.39
  403.3 0.7 copy.43
  404.0 1.0 reduce_sum.9
  405.0 0.8 slice_convert_fusion
  406.4 2.8 convert_element_type.46
  409.2 1.1 bitcast_convert_fusion
  410.4 0.7 slice_reduce_fusion
  411.2 0.7 copy.44
  411.9 0.7 copy.42
  412.6 1.3 copy.49
  413.9 1.0 copy-done
  415.0 1.3 copy.50
  (31 shorter events, 1.7 us)
Async XLA Ops:
  2.0 4.1 copy-start.4
  2.1 5.1 %copy-start.5 = (bf16[1024,4]{0,1:T(4,128)(2,1)S(1)}, bf16[1024,4]{0,1:T(4,128)(2,1)}, u32[]{:S(2)}) copy-start(bf16[1024,4]{0,1:T(4,128)(2,1)} %param.20) | copy-start | bytes 24580
  2.1 5.7 %copy-start.6 = (bf16[1024]{0:T(1024)(128)(2,1)S(1)}, bf16[1024]{0:T(1024)(128)(2,1)}, u32[]{:S(2)}) copy-start(bf16[1024]{0:T(1024)(128)(2,1)} %param.21) | copy-start | bytes 6148
  2.1 6.3 %copy-start.7 = (bf16[1024]{0:T(1024)(128)(2,1)S(1)}, bf16[1024]{0:T(1024)(128)(2,1)}, u32[]{:S(2)}) copy-start(bf16[1024]{0:T(1024)(128)(2,1)} %param.24) | copy-start | bytes 6148
  2.1 6.9 %copy-start.10 = (s32[1,256]{1,0:T(1,128)S(1)}, s32[1,256]{1,0:T(1,128)}, u32[]{:S(2)}) copy-start(s32[1,256]{1,0:T(1,128)} %param.17) | copy-start | bytes 3076
  2.1 7.9 %copy-start.9 = (bf16[512]{0:T(512)(128)(2,1)S(1)}, bf16[512]{0:T(512)(128)(2,1)}, u32[]{:S(2)}) copy-start(bf16[512]{0:T(512)(128)(2,1)} %param.18) | copy-start | bytes 3076
  10.6 147.1 %copy-start.8 = (bf16[1024]{0:T(1024)(128)(2,1)S(1)}, bf16[1024]{0:T(1024)(128)(2,1)}, u32[]{:S(2)}) copy-start(bf16[1024]{0:T(1024)(128)(2,1)} %param.26) | copy-start | bytes 6148
  401.0 8.2 %copy-start.3 = (bf16[2,64,2048]{2,1,0:T(8,128)(2,1)S(1)}, bf16[2,64,2048]{2,1,0:T(8,128)(2,1)}, u32[]{:S(2)}) copy-start(bf16[2,64,2048]{2,1,0:T(8,128)(2,1)} %get-tuple-element.77) | copy-start | bytes 1572868
  406.4 4.0 copy-start.2
  406.4 6.2 %copy-start.1 = (f32[256,2048]{1,0:T(8,128)S(1)}, f32[256,2048]{1,0:T(8,128)}, u32[]{:S(2)}) copy-start(f32[256,2048]{1,0:T(8,128)} %get-tuple-element.72) | copy-start | bytes 6291460
  412.6 2.3 copy-start
